TPU v7x, 32 devices: a whole 2x2x4 slice. The times are simulated.
32 devices in a mesh: grp: 4 (over y, x), ep: 8 (over z, core).
Axes of the slice: x: 2, y: 2, z: 4, core: 2. Of those that a mesh axis runs over, the one named last changes fastest.
Arguments:
- tokens: bfloat16 [256, 4096], P(('grp', 'ep')), may hold values from -6 to 6
- expert_ids: int32 [256, 8], P(('grp', 'ep')), may hold values from 0 to 15, all different within a row; in each aligned block of 8 rows (0 to 7, 8 to 15, ...) at most 8 rows name the same one
- gate_weights: float32 [256, 8], P(('grp', 'ep')), may hold values from 0.1 to 1
- w_gate: bfloat16 [8, 4096, 2048], P('ep', None, 'grp'), may hold values from -0.09375 to 0.09375
- w_up: bfloat16 [8, 4096, 2048], P('ep', None, 'grp'), may hold values from -0.09375 to 0.09375
- w_down: bfloat16 [8, 1024, 8192], P('ep', None, 'grp'), may hold values from -0.1875 to 0.1875
- norm_gain: float32 [4096], replicated, may hold values from 0.1 to 1.9
Outputs:
- scored: bfloat16 [256, 4096], P(('grp', 'ep'))
Inputs may be any that keep to these rules, and one draw needn't show every extreme that they name: `expert_ids`: each row names 8 different experts. Among the 8 rows of one device no expert is named by more than 8 rows, and in some devices' rows an expert is named by exactly 8.
All inputs are finite; a program needn't handle non-finite values.
Results may differ from a plain program's by a relative error of at most 0.0043.
Values may be sent and summed in bfloat16 or wider, within the bound.
A program may use at most 64 MiB of HBM per device.

v0:
```python
import jax
import jax.numpy as jnp
from jax import lax
from jax.sharding import PartitionSpec as P


def swapped(shard, axis, bit):
    return lax.ppermute(shard, axis, [(i, i ^ 1 << bit) for i in range(lax.axis_size(axis))])


def expert_front(arrived, gate_slice, up_slice):
    gate_part = jnp.einsum("abmd,df->abmf", arrived, gate_slice, preferred_element_type=jnp.float32)
    up_part = jnp.einsum("abmd,df->abmf", arrived, up_slice, preferred_element_type=jnp.float32)
    return (jax.nn.silu(gate_part) * up_part).astype(jnp.bfloat16)


def shards(tokens, expert_ids, gate_weights, w_gate, w_up, w_down, norm_gain):
    tok_rows, width = tokens.shape
    top_count = expert_ids.shape[1]
    n_ep = lax.axis_size("ep")
    n_grp = lax.axis_size("grp")
    experts = 2 * n_ep
    capacity = max(2, 2 * tok_rows * top_count // experts)
    slots = experts * capacity
    span = n_grp // 2
    flat_ids = expert_ids.reshape(-1)
    onehot = (flat_ids[:, None] == jnp.arange(experts, dtype=jnp.int32)[None, :]).astype(jnp.int32)
    earlier = jnp.cumsum(onehot, axis=0) - onehot
    ranking = jnp.sum(earlier * onehot, axis=1)
    slot_ids = jnp.arange(slots, dtype=jnp.int32)
    send_slot = flat_ids % 2 * (n_ep * capacity) + flat_ids // 2 * capacity + ranking
    placing = send_slot.reshape(tok_rows, top_count)[None, :, :] == slot_ids[:, None, None]
    placing = jnp.sum(placing.astype(jnp.float32), axis=2).astype(jnp.bfloat16)
    outgoing = jnp.dot(placing, tokens, preferred_element_type=jnp.float32).astype(jnp.bfloat16)
    outgoing = outgoing.reshape(2, n_ep, capacity, width)
    gate_slice = w_gate[0]
    up_slice = w_up[0]
    arrived = lax.all_to_all(outgoing, "ep", split_axis=1, concat_axis=1, tiled=True)
    fanned = jnp.repeat(arrived, span, axis=0)
    hidden = expert_front(
        lax.all_to_all(fanned, "grp", split_axis=0, concat_axis=0, tiled=True), gate_slice, up_slice
    )
    my_index = lax.axis_index("grp")
    assembled = hidden
    for level in range(span.bit_length() - 1):
        partner = swapped(assembled, "grp", level)
        upper = my_index // (1 << level) % 2
        assembled = jnp.where(
            upper == 0,
            jnp.concatenate([assembled, partner], axis=3),
            jnp.concatenate([partner, assembled], axis=3),
        )
    expert_out = jnp.einsum(
        "abmf,fc->abmc", assembled, w_down[0], preferred_element_type=jnp.float32
    ).astype(jnp.bfloat16)
    returned = lax.all_to_all(expert_out, "grp", split_axis=0, concat_axis=3, tiled=True)
    returned = returned.reshape(n_ep, capacity, 2, width)
    home = lax.all_to_all(returned, "ep", split_axis=0, concat_axis=0, tiled=True)
    back_slot = flat_ids // 2 * (capacity * 2) + ranking * 2 + flat_ids % 2
    matches = back_slot.reshape(tok_rows, top_count)[:, :, None] == slot_ids[None, None, :]
    weight_table = jnp.sum(jnp.where(matches, gate_weights[:, :, None], jnp.float32(0.0)), axis=1)
    combined = jnp.dot(
        weight_table,
        home.reshape(slots, width).astype(jnp.float32),
        precision=lax.Precision.HIGHEST,
    )
    mixed = tokens.astype(jnp.float32) + combined
    factor = lax.rsqrt(jnp.mean(mixed * mixed, axis=1, keepdims=True) + 1e-06)
    return (mixed * factor * norm_gain).astype(jnp.bfloat16)


def solution(mesh):
    placed = (
        P(("grp", "ep"), None),
        P(("grp", "ep"), None),
        P(("grp", "ep"), None),
        P("ep", None, "grp"),
        P("ep", None, "grp"),
        P("ep", None, "grp"),
        P(),
    )
    return jax.shard_map(
        shards, mesh=mesh, in_specs=placed, out_specs=P(("grp", "ep"), None), check_vma=False
    )
```

profile of v0, /device:TPU:0, one launch (start us, length us, event | category | flops | bytes accessed | tf_op | source)
XLA Modules:
  0.0 127.7 jit_solution(3997107952723632607)
XLA Ops:
  0.0 0.8 eq.49
  0.8 0.1 reduce_window_sum.11
  0.9 0.2 select_reduce_fusion.1
  1.2 0.7 add_add_fusion
  1.9 0.1 convert_reduce_fusion
  2.0 1.3 %convolution_convert_fusion = bf16[128,4096]{1,0:T(8,128)(2,1)S(1)} fusion(bf16[8,4096]{1,0:T(8,128)(2,1)} %param.7, bf16[128,8]{0,1:T(8,128)(2,1)S(1)} %convert_reduce_fusion), kind=kOutput, calls=%fused_computation | convolution fusion | flops 8912896 | bytes 1116160 | tf_op jit(solution)/shard_map/dot_general | solution.py:34
  3.3 0.1 copy.12
  3.4 32.7 %all_to_all.30 = bf16[2,8,8,4096]{3,2,0,1:T(8,128)(2,1)S(1)} all-to-all(bf16[2,8,8,4096]{3,2,0,1:T(8,128)(2,1)S(1)} %copy.12), channel_id=1, replica_groups=mesh['grp'=4,'ep'=8] {'ep'}, dimensions={1} | all-to-all | bytes 2097152 | tf_op jit(solution)/shard_map/all_to_all | solution.py:38
  36.2 0.2 broadcast_in_dim.23
  36.5 28.8 %all_to_all.31 = bf16[4,8,8,4096]{3,2,1,0:T(8,128)(2,1)S(1)} all-to-all(bf16[4,8,8,4096]{3,2,1,0:T(8,128)(2,1)S(1)} %bitcast.38), channel_id=1, replica_groups=mesh['grp'=4,'ep'=8] {'grp'}, dimensions={0} | all-to-all | bytes 4194304 | tf_op jit(solution)/shard_map/all_to_all | solution.py:41
  65.3 1.2 fusion.4
  66.5 0.9 copy-done.4
  67.4 1.3 fusion.12
  68.7 1.0 collective-permute-start
  69.7 5.5 %collective-permute-done = bf16[4,8,8,512]{3,2,1,0:T(8,128)(2,1)S(1)} collective-permute-done((bf16[4,8,8,512]{3,2,1,0:T(8,128)(2,1)S(1)}, bf16[4,8,8,512]{3,2,1,0:T(8,128)(2,1)S(1)}, u32[]{:S(2)}, u32[]{:S(2)}) %collective-permute-start) | collective-permute-done | bytes 262176 | tf_op jit(solution)/shard_map/ppermute | solution.py:8
  75.2 3.5 %fusion.6 = bf16[4,8,8,2048]{3,2,1,0:T(8,128)(2,1)S(1)} fusion(bf16[1,1024,2048]{2,1,0:T(8,128)(2,1)} %param.12, bf16[4,8,8,512]{3,2,1,0:T(8,128)(2,1)S(1)} %collective-permute-done, bf16[4,8,8,512]{3,2,1,0:T(8,128)(2,1)S(1)} %fusion.12, pred[]{:T(512)S(6)} %eq.56), kind=kOutput, calls=%fused_computation.8 | convolution fusion | flops 1076625408 | bytes 5767169 | tf_op jit(solution)/shard_map/abmf,fc->abmc/dot_general | solution.py:53
  78.6 13.7 %all_to_all.32 = bf16[4,8,8,2048]{3,2,1,0:T(8,128)(2,1)S(1)} all-to-all(bf16[4,8,8,2048]{3,2,1,0:T(8,128)(2,1)S(1)} %fusion.6), channel_id=1, replica_groups=mesh['grp'=4,'ep'=8] {'grp'}, dimensions={0} | all-to-all | bytes 2097152 | tf_op jit(solution)/shard_map/all_to_all | solution.py:56
  92.4 0.8 copy.14
  93.2 1.6 %reshape.95 = bf16[8,8,2,4096]{3,2,1,0:T(2,128)(2,1)} reshape(bf16[1,8,8,4,2048]{4,3,2,1,0:T(4,128)(2,1)S(1)} %copy.14) | data formatting | bytes 2097152 | tf_op jit(solution)/shard_map/reshape | solution.py:57
  94.8 4.5 %all-to-all-start.3 = ((bf16[8,8,2,4096]{3,2,1,0:T(2,128)(2,1)}), bf16[8,8,2,4096]{3,2,1,0:T(2,128)(2,1)S(1)}, u32[]{:S(2)}, u32[]{:S(2)}) async-start(bf16[8,8,2,4096]{3,2,1,0:T(2,128)(2,1)} %reshape.95), calls=%async_computation.3 | async-start | bytes 2097152 | tf_op jit(solution)/shard_map/all_to_all | solution.py:58
  99.4 26.5 %all-to-all-done.3 = bf16[8,8,2,4096]{3,2,1,0:T(2,128)(2,1)S(1)} async-done(((bf16[8,8,2,4096]{3,2,1,0:T(2,128)(2,1)}), bf16[8,8,2,4096]{3,2,1,0:T(2,128)(2,1)S(1)}, u32[]{:S(2)}, u32[]{:S(2)}) %all-to-all-start.3) | async-done | bytes 1048608 | tf_op jit(solution)/shard_map/all_to_all | solution.py:58
  125.9 0.4 reshape.96
  126.4 0.6 multiply_reduce_fusion
  127.0 0.7 multiply_convert_fusion
  (14 shorter events, 0.3 us)
Async XLA Ops:
  36.2 29.0 %copy-start.3 = (bf16[1,4096,512]{2,1,0:T(8,128)(2,1)S(1)}, bf16[1,4096,512]{2,1,0:T(8,128)(2,1)}, u32[]{:S(2)}) copy-start(bf16[1,4096,512]{2,1,0:T(8,128)(2,1)} %param.10) | copy-start | bytes 12582916
  65.3 2.2 %copy-start.4 = (bf16[1,4096,512]{2,1,0:T(8,128)(2,1)S(1)}, bf16[1,4096,512]{2,1,0:T(8,128)(2,1)}, u32[]{:S(2)}) copy-start(bf16[1,4096,512]{2,1,0:T(8,128)(2,1)} %param.11) | copy-start | bytes 12582916
  68.7 6.4 %collective-permute-start = (bf16[4,8,8,512]{3,2,1,0:T(8,128)(2,1)S(1)}, bf16[4,8,8,512]{3,2,1,0:T(8,128)(2,1)S(1)}, u32[]{:S(2)}, u32[]{:S(2)}) collective-permute-start(bf16[4,8,8,512]{3,2,1,0:T(8,128)(2,1)S(1)} %fusion.12), channel_id=1, source_target_pairs={{0,8},{8,0},{16,24},{24,16},{1,9},{9,1},{17,25},{25,17},{2,10},{10... | collective-permute-start | bytes 786440 | tf_op jit(solution)/shard_map/ppermute | solution.py:8
  78.6 20.7 %copy-start.2 = (f32[8,8]{1,0:T(8,128)S(1)}, f32[8,8]{1,0:T(8,128)}, u32[]{:S(2)}) copy-start(f32[8,8]{1,0:T(8,128)} %param.9) | copy-start | bytes 772
  92.4 34.0 %copy-start = (bf16[8,4096]{1,0:T(8,128)(2,1)S(1)}, bf16[8,4096]{1,0:T(8,128)(2,1)}, u32[]{:S(2)}) copy-start(bf16[8,4096]{1,0:T(8,128)(2,1)} %param.7) | copy-start | bytes 196612
  93.2 33.8 %copy-start.1 = (f32[4096]{0:T(1024)S(1)}, f32[4096]{0:T(1024)}, u32[]{:S(2)}) copy-start(f32[4096]{0:T(1024)} %param.13) | copy-start | bytes 49156
  94.8 31.1 %all-to-all-start.3 = ((bf16[8,8,2,4096]{3,2,1,0:T(2,128)(2,1)}), bf16[8,8,2,4096]{3,2,1,0:T(2,128)(2,1)S(1)}, u32[]{:S(2)}, u32[]{:S(2)}) async-start(bf16[8,8,2,4096]{3,2,1,0:T(2,128)(2,1)} %reshape.95), calls=%async_computation.3 | async-start | bytes 2097152 | tf_op jit(solution)/shard_map/all_to_all | solution.py:58
where the time goes:
time: 128 us
  blocking collectives  75.2 us (59%)
  waiting for transfers between devices  32 us (25%)
  matrix products  7.91 us (6%)
  starting transfers between devices  5.46 us (4%)
  local copies, waits for them, and re-layouts  5.07 us (4%)
  other arithmetic  1.97 us (2%)
    all_to_all x1, blocking collectives, shards(): lax.all_to_all(outgoing, 'ep', split_axis=1, concat_axis=1, tiled=True)  32.7 us
    all_to_all x1, blocking collectives, shards(): lax.all_to_all(fanned, 'grp', split_axis=0, concat_axis=0, tiled=True)  28.8 us
    all_to_all x1, waiting for transfers between devices, shards(): lax.all_to_all(returned, 'ep', split_axis=0, concat_axis=0, tiled=True)  26.5 us
    all_to_all x1, blocking collectives, shards(): lax.all_to_all(expert_out, 'grp', split_axis=0, concat_axis=3, tiled=True)  13.7 us
    ppermute x1, waiting for transfers between devices, swapped(): lax.ppermute(shard, axis, [(i, i ^ 1 << bit) for i in range(lax.axis_size...  5.46 us
    all_to_all x1, starting transfers between devices, shards(): lax.all_to_all(returned, 'ep', split_axis=0, concat_axis=0, tiled=True)  4.48 us
    dot_general x1, matrix products, shards(): jnp.einsum('abmf,fc->abmc', assembled, w_down[0], preferred_element_type=...  3.46 us
  transfers between devices with their start and end apart: 2, of which 2 were waited for; matrix products, arithmetic and copies ran while one was open for 0% of the time, Pallas kernels for 0%

commit v1 on v0

--- a/solution.py
+++ b/solution.py
@@ -1,7 +1,289 @@
+import functools
+
 import jax
 import jax.numpy as jnp
 from jax import lax
+from jax.experimental import pallas as pl
+from jax.experimental.pallas import tpu as pltpu
 from jax.sharding import PartitionSpec as P
+
+LANES = 128
+MESH = pl.DeviceIdType.MESH
+
+
+def dot32(a, b):
+    return jnp.dot(a, b, preferred_element_type=jnp.float32)
+
+
+def fused_kernel(
+    nz, experts,
+    tok_ref, ids_ref, gates_ref, gain_ref, wg_hbm, wu_hbm, wd_hbm, out_ref,
+    wg, wu, wd, s_out, s_in, xm, xs, hid_out, hid_in, part_out, part_in, ret_out, ret_in, fin_out, fin_in,
+    w_sem, s_sem, z_sem, x_sem, y_sem, dx_sem, dy_sem, sib_sem, hid_sem, part_sem, ret_sem, fin_sem,
+):
+    f32, bf16 = jnp.float32, jnp.bfloat16
+    rows, width = tok_ref.shape
+    half = width // 2
+    quarter = width // 4
+    block = 2 * rows
+    column = nz * block
+    ff_half = wg.shape[2]
+    g, p = lax.axis_index("grp"), lax.axis_index("ep")
+    y, x = g // 2, g % 2
+    z, c = p // 2, p % 2
+    ox, oy, oc = 1 - x, 1 - y, 1 - c
+
+    def dev(xx, yy, zz, cc):
+        return (yy * 2 + xx, zz * 2 + cc)
+
+    def remote(src, dst, sems, idx, to):
+        return pltpu.make_async_remote_copy(
+            src_ref=src, dst_ref=dst, send_sem=sems.at[0, idx], recv_sem=sems.at[1, idx],
+            device_id=to, device_id_type=MESH,
+        )
+
+    sibling = dev(x, y, z, oc)
+    x_peer = dev(ox, y, z, c)
+    y_peer = dev(x, oy, z, c)
+
+    loads = []
+    n = 0
+    for mine, at_k in ((0, c), (1, oc)):
+        for src, dst in ((wg_hbm, wg), (wu_hbm, wu)):
+            span = pl.ds(pl.multiple_of(at_k * half, half), half)
+            loads.append(pltpu.make_async_copy(src.at[0, span, :], dst.at[mine], w_sem.at[n]))
+            n += 1
+    for mine, at_k in ((0, x), (1, ox)):
+        span = pl.ds(pl.multiple_of(at_k * ff_half, ff_half), ff_half)
+        loads.append(pltpu.make_async_copy(wd_hbm.at[0, span, :], wd.at[mine], w_sem.at[n]))
+        n += 1
+
+    barrier = pltpu.get_barrier_semaphore()
+    greeted = 0
+    for dy in range(2):
+        for dx in range(2):
+            for dz in range(nz):
+                if dy or dx or dz:
+                    to = dev((x + dx) % 2, (y + dy) % 2, (z + dz) % nz, c)
+                    pl.semaphore_signal(barrier, inc=1, device_id=to, device_id_type=MESH)
+                    greeted += 1
+    pl.semaphore_signal(barrier, inc=1, device_id=sibling, device_id_type=MESH)
+    greeted += 1
+    for load in loads:
+        load.start()
+
+    lane = lax.broadcasted_iota(jnp.int32, (rows, LANES), 1)
+    table = jnp.zeros((rows, LANES), f32)
+    for k in range(ids_ref.shape[1]):
+        table += jnp.where(ids_ref[:, k : k + 1] == lane % experts, gates_ref[:, k : k + 1], f32(0.0))
+    tok = tok_ref[...].astype(f32)
+    first = c == 0
+    mine_half = jnp.where(first, tok[:, :half], tok[:, half:])
+    s_out[:, :half] = jnp.where(first, tok[:, half:], tok[:, :half])
+    s_out[:, half:] = table
+    pl.semaphore_wait(barrier, greeted)
+
+    sends = []
+
+    def go(copy):
+        copy.start()
+        sends.append(copy)
+        return copy
+
+    swap = go(remote(s_out, s_in, s_sem, 0, sibling))
+    swap.wait_recv()
+    theirs, their_table = s_in[:, :half], s_in[:, half:]
+
+    def both(a, b):
+        return jnp.where(first, jnp.concatenate([a, b], axis=0), jnp.concatenate([b, a], axis=0))
+
+    pair_table = both(table, their_table)
+    high = pair_table.astype(bf16)
+    rest = pair_table - high.astype(f32)
+    middle = rest.astype(bf16)
+    low = (rest - middle.astype(f32)).astype(bf16)
+    part = lax.broadcasted_iota(jnp.int32, (block, LANES), 1) // experts
+    coded = jnp.where(
+        part == 0, high.astype(f32),
+        jnp.where(part == 1, middle.astype(f32), jnp.where(part == 2, low.astype(f32), f32(0.0))),
+    )
+
+    def spot(xx, i):
+        return pl.ds(pl.multiple_of(xx * column + i * block, block), block)
+
+    def whole(xx):
+        return pl.ds(pl.multiple_of(xx * column, column), column)
+
+    xm[0, spot(x, 0), :] = jnp.concatenate([both(mine_half, theirs), coded], axis=1).astype(bf16)
+
+    z_copy = [None] + [
+        remote(xm.at[0, spot(x, 0), :], xm.at[0, spot(x, i), :], z_sem, i, dev(x, y, (z + i) % nz, c))
+        for i in range(1, nz)
+    ]
+    x_copy = [remote(xm.at[0, spot(x, i), :], xm.at[0, spot(x, i), :], x_sem, i, x_peer) for i in range(nz)]
+    x_land = [remote(xm.at[0, spot(ox, i), :], xm.at[0, spot(ox, i), :], x_sem, i, x_peer) for i in range(nz)]
+    y_copy = [remote(xm.at[0, spot(x, i), :], xm.at[1, spot(x, i), :], y_sem, i, y_peer) for i in range(nz)]
+    by_y = [i for i in range(nz) if i % 4 in (1, 2)]
+    d_copy, d_land = [], []
+    for i in range(nz):
+        if i in by_y:
+            d_copy.append(remote(xm.at[0, spot(ox, i), :], xm.at[1, spot(ox, i), :], dy_sem, i, y_peer))
+            d_land.append(d_copy[-1])
+        else:
+            d_copy.append(remote(xm.at[1, spot(x, i), :], xm.at[1, spot(x, i), :], dx_sem, i, x_peer))
+            d_land.append(remote(xm.at[1, spot(ox, i), :], xm.at[1, spot(ox, i), :], dx_sem, i, x_peer))
+    sib_copy = [
+        [remote(xm.at[s, whole(xx), :], xs.at[s, whole(xx), :], sib_sem, 2 * s + j, sibling)
+         for j, xx in enumerate((x, ox))]
+        for s in range(2)
+    ]
+
+    for i in range(1, nz):
+        go(z_copy[i])
+    go(x_copy[0])
+    go(y_copy[0])
+    for i in range(1, nz):
+        z_copy[i].wait_recv()
+        go(x_copy[i])
+        go(y_copy[i])
+    go(sib_copy[0][0])
+    for i in range(nz):
+        x_land[i].wait_recv()
+        if i in by_y:
+            go(d_copy[i])
+        y_copy[i].wait_recv()
+        if i not in by_y:
+            go(d_copy[i])
+    go(sib_copy[0][1])
+    go(sib_copy[1][0])
+
+    def front(s):
+        gate = dot32(xm[s, :, :half], wg[0])
+        up = dot32(xm[s, :, :half], wu[0])
+        if s == 0:
+            for load in loads[2:4]:
+                load.wait()
+        for j in range(2):
+            sib_copy[s][j].wait_recv()
+        gate += dot32(xs[s, :, :half], wg[1])
+        up += dot32(xs[s, :, :half], wu[1])
+        hid_out[s] = (gate / (f32(1.0) + jnp.exp(-gate)) * up).astype(bf16)
+
+    hid_copy = [remote(hid_out.at[s], hid_in.at[s], hid_sem, s, x_peer) for s in range(2)]
+    for load in loads[:2]:
+        load.wait()
+    front(0)
+    go(hid_copy[0])
+    for i in range(nz):
+        d_land[i].wait_recv()
+    go(sib_copy[1][1])
+    front(1)
+    go(hid_copy[1])
+
+    for load in loads[4:]:
+        load.wait()
+    part_copy = [remote(part_out.at[s], part_in.at[s], part_sem, s, sibling) for s in range(2)]
+    lanes = lax.broadcasted_iota(jnp.int32, (2 * column, LANES), 1)
+    wanted = (lanes % experts == 2 * p + y) & (lanes < 3 * experts)
+
+    def ret_copy(s, j, i):
+        to = dev((ox if j else x), (oy if s else y), (z + nz - i) % nz, c)
+        slot = (s * 2 + j) * nz + i
+        return remote(ret_out.at[s, spot(ox if j else x, i), :], ret_in.at[slot], ret_sem, slot, to)
+
+    def back(s):
+        weight = jnp.sum(jnp.where(wanted, xm[s, :, half:].astype(f32), f32(0.0)), axis=1, keepdims=True)
+        hid_copy[s].wait_recv()
+
+        def quarter_of(which):
+            cols = pl.ds(pl.multiple_of(which * quarter, quarter), quarter)
+            return (dot32(hid_out[s], wd[0, :, cols]) + dot32(hid_in[s], wd[1, :, cols])) * weight
+
+        part_out[s] = quarter_of(oc).astype(bf16)
+        go(part_copy[s])
+        own = quarter_of(c)
+        part_copy[s].wait_recv()
+        ret_out[s] = (own + part_in[s].astype(f32)).astype(bf16)
+        for i in (2, 1, 3, 0) if nz == 4 else range(nz):
+            for j in (1, 0):
+                if s or j or i:
+                    go(ret_copy(s, j, i))
+
+    back(0)
+    back(1)
+
+    sums = [jnp.zeros((block, quarter), f32), jnp.zeros((block, quarter), f32)]
+    sums[0] += ret_out[0, spot(x, 0), :].astype(f32)
+    for s in range(2):
+        for i in range(nz):
+            for j in range(2):
+                if s or j or i:
+                    ret_copy(s, j, i).wait_recv()
+                    sums[j] += ret_in[(s * 2 + j) * nz + i].astype(f32)
+    for j in range(2):
+        fin_out[:, j * quarter : (j + 1) * quarter] = jnp.where(first, sums[j][rows:], sums[j][:rows])
+    fin = go(remote(fin_out, fin_in, fin_sem, 0, sibling))
+    mine = [jnp.where(first, sums[j][:rows], sums[j][rows:]) for j in range(2)]
+    fin.wait_recv()
+    other = [fin_in[:, j * quarter : (j + 1) * quarter] for j in range(2)]
+    pieces = []
+    for h in range(2):
+        for q in range(2):
+            near = jnp.where(c == q, mine[0], other[0])
+            far = jnp.where(c == q, mine[1], other[1])
+            pieces.append(jnp.where(x == h, near, far))
+    mixed = tok_ref[...].astype(f32) + jnp.concatenate(pieces, axis=1)
+    factor = lax.rsqrt(jnp.mean(mixed * mixed, axis=1, keepdims=True) + 1e-06)
+    out_ref[...] = (mixed * factor * gain_ref[...]).astype(bf16)
+    for copy in sends:
+        copy.wait_send()
+
+
+def fused(tokens, expert_ids, gate_weights, w_gate, w_up, w_down, norm_gain):
+    f32, bf16 = jnp.float32, jnp.bfloat16
+    rows, width = tokens.shape
+    n_ep = lax.axis_size("ep")
+    nz, experts = n_ep // 2, 2 * n_ep
+    half, quarter = width // 2, width // 4
+    block = 2 * rows
+    stage = 2 * nz * block
+    wide = half + LANES
+    ff_half, out_cols = w_gate.shape[2], w_down.shape[2]
+    vmem = pltpu.VMEM
+
+    def sems(count):
+        return pltpu.SemaphoreType.DMA((2, count))
+
+    whole = pl.BlockSpec(memory_space=pltpu.VMEM)
+    return pl.pallas_call(
+        functools.partial(fused_kernel, nz, experts),
+        out_shape=jax.ShapeDtypeStruct((rows, width), bf16),
+        in_specs=[whole] * 4 + [pl.BlockSpec(memory_space=pl.ANY)] * 3,
+        out_specs=whole,
+        scratch_shapes=[
+            vmem((2, half, ff_half), bf16),
+            vmem((2, half, ff_half), bf16),
+            vmem((2, ff_half, out_cols), bf16),
+            vmem((rows, wide), f32),
+            vmem((rows, wide), f32),
+            vmem((2, stage, wide), bf16),
+            vmem((2, stage, wide), bf16),
+            vmem((2, stage, ff_half), bf16),
+            vmem((2, stage, ff_half), bf16),
+            vmem((2, stage, quarter), bf16),
+            vmem((2, stage, quarter), bf16),
+            vmem((2, stage, quarter), bf16),
+            vmem((4 * nz, block, quarter), bf16),
+            vmem((rows, half), f32),
+            vmem((rows, half), f32),
+            pltpu.SemaphoreType.DMA((6,)),
+            sems(1), sems(nz), sems(nz), sems(nz), sems(nz), sems(nz), sems(4), sems(2), sems(2),
+            sems(4 * nz), sems(1),
+        ],
+        compiler_params=pltpu.CompilerParams(
+            collective_id=0, has_side_effects=True, vmem_limit_bytes=48 * 1024 * 1024
+        ),
+    )(tokens, expert_ids, gate_weights, norm_gain.reshape(1, width), w_gate, w_up, w_down)
 
 
 def swapped(shard, axis, bit):
@@ -14,7 +296,7 @@
     return (jax.nn.silu(gate_part) * up_part).astype(jnp.bfloat16)
 
 
-def shards(tokens, expert_ids, gate_weights, w_gate, w_up, w_down, norm_gain):
+def routed(tokens, expert_ids, gate_weights, w_gate, w_up, w_down, norm_gain):
     tok_rows, width = tokens.shape
     top_count = expert_ids.shape[1]
     n_ep = lax.axis_size("ep")
@@ -69,6 +351,12 @@
     return (mixed * factor * norm_gain).astype(jnp.bfloat16)
 
 
+def shards(tokens, *rest):
+    all_rows = tokens.shape[0] * lax.axis_size("grp") * lax.axis_size("ep")
+    dense = lax.axis_size("grp") == 4 and lax.axis_size("ep") % 2 == 0 and all_rows <= 256
+    return (fused if dense else routed)(tokens, *rest)
+
+
 def solution(mesh):
     placed = (
         P(("grp", "ep"), None),

time: 128 us -> 50.7 us (0.40)
  blocking collectives: 75.2 us -> 0 us
  Pallas kernels: 0 us -> 44.6 us
  waiting for transfers between devices: 32 us -> 0 us
  matrix products: 7.91 us -> 0 us
  starting transfers between devices: 5.46 us -> 0 us
  other arithmetic: 1.97 us -> 0 us
    all_to_all x3 -> x0, blocking collectives: 75.2 us -> none  [the longest x1 32.7 us: shards(): lax.all_to_all(outgoing, 'ep', split_axis=1, concat_axis=1, tiled=True)]
    pallas_call x0 -> x1, Pallas kernels: none -> 44.6 us  [fused(): pl.pallas_call(functools.partial(fused_kernel, nz, experts), out_shape=ja...]
    all_to_all x1 -> x0, waiting for transfers between devices: 26.5 us -> none  [shards(): lax.all_to_all(returned, 'ep', split_axis=0, concat_axis=0, tiled=True)]
    dot_general x5 -> x0, matrix products: 7.91 us -> none  [the longest x1 3.46 us: shards(): jnp.einsum('abmf,fc->abmc', assembled, w_down[0], preferred_element_type=...]
    ppermute x1 -> x0, waiting for transfers between devices: 5.46 us -> none  [swapped(): lax.ppermute(shard, axis, [(i, i ^ 1 << bit) for i in range(lax.axis_size...]
    unnamed x10 -> x11, local copies, waits for them, and re-layouts: 0.97 us -> 5.75 us
    all_to_all x1 -> x0, starting transfers between devices: 4.48 us -> none  [shards(): lax.all_to_all(returned, 'ep', split_axis=0, concat_axis=0, tiled=True)]
    reshape x3 -> x0, local copies, waits for them, and re-layouts: 2.14 us -> none  [the longest x1 1.63 us: shards(): returned = returned.reshape(n_ep, capacity, 2, width)]
  transfers between devices with their start and end apart: 2 -> 0, of which waited for: 2 -> 0; matrix products, arithmetic and copies ran while one was open for 0% -> 0% of each run, Pallas kernels for 0% -> 0%
where the time goes in v1:
time: 50.7 us; the launch traced here: 50.4 us
  Pallas kernels  44.6 us (88%)
  local copies, waits for them, and re-layouts  5.75 us (11%)
    pallas_call x1, Pallas kernels, fused(): pl.pallas_call(functools.partial(fused_kernel, nz, experts), out_shape=ja...  44.6 us
    unnamed x11, local copies, waits for them, and re-layouts  5.75 us

profile of v1, /device:TPU:0, one launch (start us, length us, event | category | flops | bytes accessed | tf_op | source)
XLA Modules:
  0.0 50.4 jit_solution(13166524387091340117)
XLA Ops:
  0.0 0.0 copy-start
  0.0 2.2 %copy-done = bf16[1,4096,512]{2,1,0:T(8,128)(2,1)S(1)} copy-done((bf16[1,4096,512]{2,1,0:T(8,128)(2,1)S(1)}, bf16[1,4096,512]{2,1,0:T(8,128)(2,1)}, u32[]{:S(2)}) %copy-start) | copy-done | bytes 4194328
  2.2 0.0 copy-start.1
  2.2 0.8 %copy-done.1 = bf16[8,4096]{1,0:T(8,128)(2,1)S(1)} copy-done((bf16[8,4096]{1,0:T(8,128)(2,1)S(1)}, bf16[8,4096]{1,0:T(8,128)(2,1)}, u32[]{:S(2)}) %copy-start.1) | copy-done | bytes 65560
  3.0 0.0 copy-start.2
  3.0 0.7 %copy-done.2 = f32[4096]{0:T(1024)S(1)} copy-done((f32[4096]{0:T(1024)S(1)}, f32[4096]{0:T(1024)}, u32[]{:S(2)}) %copy-start.2) | copy-done | bytes 16408
  3.7 0.0 copy-start.3
  3.7 0.7 %copy-done.3 = s32[8,8]{1,0:T(8,128)S(1)} copy-done((s32[8,8]{1,0:T(8,128)S(1)}, s32[8,8]{1,0:T(8,128)}, u32[]{:S(2)}) %copy-start.3) | copy-done | bytes 280
  4.4 0.0 copy-start.4
  4.4 0.7 %copy-done.4 = f32[8,8]{1,0:T(8,128)S(1)} copy-done((f32[8,8]{1,0:T(8,128)S(1)}, f32[8,8]{1,0:T(8,128)}, u32[]{:S(2)}) %copy-start.4) | copy-done | bytes 280
  5.1 44.6 %shard_map.73 = bf16[8,4096]{1,0:T(8,128)(2,1)S(1)} custom-call(bf16[8,4096]{1,0:T(8,128)(2,1)S(1)} %copy-done.1, s32[8,8]{1,0:T(8,128)S(1)} %copy-done.3, f32[8,8]{1,0:T(8,128)S(1)} %copy-done.4, f32[1,4096]{1,0:T(1,128)S(1)} %bitcast.1, bf16[1,4096,512]{2,1,0:T(8,128)(2,1)S(1)} %copy-done, bf16[1,4096,512]{2,1,0:T(8,128)(2,1)} %wu_hbm.1, ...), custom_call_target="tpu_custom_call" | custom-call | tf_op jit(solution)/shard_map/pallas_call | solution.py:258
  49.7 0.6 %copy.9 = bf16[8,4096]{1,0:T(8,128)(2,1)} copy(bf16[8,4096]{1,0:T(8,128)(2,1)S(1)} %shard_map.73) | data formatting | bytes 131072
Async XLA Ops:
  0.0 2.2 %copy-start = (bf16[1,4096,512]{2,1,0:T(8,128)(2,1)S(1)}, bf16[1,4096,512]{2,1,0:T(8,128)(2,1)}, u32[]{:S(2)}) copy-start(bf16[1,4096,512]{2,1,0:T(8,128)(2,1)} %wg_hbm.1) | copy-start | bytes 12582916
  2.2 0.8 %copy-start.1 = (bf16[8,4096]{1,0:T(8,128)(2,1)S(1)}, bf16[8,4096]{1,0:T(8,128)(2,1)}, u32[]{:S(2)}) copy-start(bf16[8,4096]{1,0:T(8,128)(2,1)} %tok_ref.1) | copy-start | bytes 196612
  3.0 0.7 %copy-start.2 = (f32[4096]{0:T(1024)S(1)}, f32[4096]{0:T(1024)}, u32[]{:S(2)}) copy-start(f32[4096]{0:T(1024)} %param.13) | copy-start | bytes 49156
  3.7 0.7 %copy-start.3 = (s32[8,8]{1,0:T(8,128)S(1)}, s32[8,8]{1,0:T(8,128)}, u32[]{:S(2)}) copy-start(s32[8,8]{1,0:T(8,128)} %ids_ref.1) | copy-start | bytes 772
  4.4 0.7 %copy-start.4 = (f32[8,8]{1,0:T(8,128)S(1)}, f32[8,8]{1,0:T(8,128)}, u32[]{:S(2)}) copy-start(f32[8,8]{1,0:T(8,128)} %gates_ref.1) | copy-start | bytes 772

commit v2 on v1

--- a/solution.py
+++ b/solution.py
@@ -17,16 +17,17 @@
 
 def fused_kernel(
     nz, experts,
-    tok_ref, ids_ref, gates_ref, gain_ref, wg_hbm, wu_hbm, wd_hbm, out_ref,
-    wg, wu, wd, s_out, s_in, xm, xs, hid_out, hid_in, part_out, part_in, ret_out, ret_in, fin_out, fin_in,
-    w_sem, s_sem, z_sem, x_sem, y_sem, dx_sem, dy_sem, sib_sem, hid_sem, part_sem, ret_sem, fin_sem,
+    tok_hbm, ids_hbm, gates_hbm, gain_hbm, wg_hbm, wu_hbm, wd_hbm, out_ref,
+    tok_ref, ids_ref, gates_ref, gain_ref, wg, wu, wd, s_out, s_in, xm, xs, hid_out, hid_in, part_out, part_in, ret_out, ret_in, fin_out, fin_in,
+    t_sem, w_sem, s_sem, z_sem, x_sem, y_sem, dx_sem, dy_sem, sib_sem, hid_sem, part_sem, ret_sem, fin_sem,
 ):
     f32, bf16 = jnp.float32, jnp.bfloat16
     rows, width = tok_ref.shape
     half = width // 2
     quarter = width // 4
     block = 2 * rows
-    column = nz * block
+    stage = 2 * nz * block
+    piece = quarter // 2
     ff_half = wg.shape[2]
     g, p = lax.axis_index("grp"), lax.axis_index("ep")
     y, x = g // 2, g % 2
@@ -45,6 +46,16 @@
     sibling = dev(x, y, z, oc)
     x_peer = dev(ox, y, z, c)
     y_peer = dev(x, oy, z, c)
+    x_sibling = dev(ox, y, z, oc)
+
+    small = [
+        pltpu.make_async_copy(src, dst, t_sem.at[n])
+        for n, (src, dst) in enumerate(
+            ((tok_hbm, tok_ref), (ids_hbm, ids_ref), (gates_hbm, gates_ref), (gain_hbm, gain_ref))
+        )
+    ]
+    for load in small:
+        load.start()
 
     loads = []
     n = 0
@@ -60,15 +71,13 @@
 
     barrier = pltpu.get_barrier_semaphore()
     greeted = 0
-    for dy in range(2):
-        for dx in range(2):
-            for dz in range(nz):
-                if dy or dx or dz:
-                    to = dev((x + dx) % 2, (y + dy) % 2, (z + dz) % nz, c)
-                    pl.semaphore_signal(barrier, inc=1, device_id=to, device_id_type=MESH)
-                    greeted += 1
-    pl.semaphore_signal(barrier, inc=1, device_id=sibling, device_id_type=MESH)
-    greeted += 1
+    for to in [dev(x, (y + dy) % 2, (z + dz) % nz, c) for dy in range(2) for dz in range(nz) if dy or dz] + [
+        x_peer, sibling, x_sibling
+    ]:
+        pl.semaphore_signal(barrier, inc=1, device_id=to, device_id_type=MESH)
+        greeted += 1
+    for load in small:
+        load.wait()
     for load in loads:
         load.start()
 
@@ -109,10 +118,10 @@
     )
 
     def spot(xx, i):
-        return pl.ds(pl.multiple_of(xx * column + i * block, block), block)
-
-    def whole(xx):
-        return pl.ds(pl.multiple_of(xx * column, column), column)
+        return pl.ds(pl.multiple_of((2 * i + xx) * block, block), block)
+
+    def pair(i):
+        return slice(2 * i * block, 2 * (i + 1) * block)
 
     xm[0, spot(x, 0), :] = jnp.concatenate([both(mine_half, theirs), coded], axis=1).astype(bf16)
 
@@ -133,8 +142,7 @@
             d_copy.append(remote(xm.at[1, spot(x, i), :], xm.at[1, spot(x, i), :], dx_sem, i, x_peer))
             d_land.append(remote(xm.at[1, spot(ox, i), :], xm.at[1, spot(ox, i), :], dx_sem, i, x_peer))
     sib_copy = [
-        [remote(xm.at[s, whole(xx), :], xs.at[s, whole(xx), :], sib_sem, 2 * s + j, sibling)
-         for j, xx in enumerate((x, ox))]
+        [remote(xm.at[s, pair(i), :], xs.at[s, pair(i), :], sib_sem, s * nz + i, sibling) for i in range(nz)]
         for s in range(2)
     ]
 
@@ -142,20 +150,18 @@
         go(z_copy[i])
     go(x_copy[0])
     go(y_copy[0])
-    for i in range(1, nz):
-        z_copy[i].wait_recv()
-        go(x_copy[i])
-        go(y_copy[i])
-    go(sib_copy[0][0])
     for i in range(nz):
+        if i + 1 < nz:
+            z_copy[i + 1].wait_recv()
+            go(x_copy[i + 1])
+            go(y_copy[i + 1])
         x_land[i].wait_recv()
         if i in by_y:
             go(d_copy[i])
+        go(sib_copy[0][i])
         y_copy[i].wait_recv()
         if i not in by_y:
             go(d_copy[i])
-    go(sib_copy[0][1])
-    go(sib_copy[1][0])
 
     def front(s):
         gate = dot32(xm[s, :, :half], wg[0])
@@ -163,8 +169,8 @@
         if s == 0:
             for load in loads[2:4]:
                 load.wait()
-        for j in range(2):
-            sib_copy[s][j].wait_recv()
+        for i in range(nz):
+            sib_copy[s][i].wait_recv()
         gate += dot32(xs[s, :, :half], wg[1])
         up += dot32(xs[s, :, :half], wu[1])
         hid_out[s] = (gate / (f32(1.0) + jnp.exp(-gate)) * up).astype(bf16)
@@ -176,63 +182,74 @@
     go(hid_copy[0])
     for i in range(nz):
         d_land[i].wait_recv()
-    go(sib_copy[1][1])
+        go(sib_copy[1][i])
     front(1)
     go(hid_copy[1])
 
     for load in loads[4:]:
         load.wait()
-    part_copy = [remote(part_out.at[s], part_in.at[s], part_sem, s, sibling) for s in range(2)]
-    lanes = lax.broadcasted_iota(jnp.int32, (2 * column, LANES), 1)
+    part_copy = [
+        [remote(part_out.at[s, e], part_in.at[s, e], part_sem, 2 * s + e, sibling) for e in range(2)]
+        for s in range(2)
+    ]
+    lanes = lax.broadcasted_iota(jnp.int32, (stage, LANES), 1)
     wanted = (lanes % experts == 2 * p + y) & (lanes < 3 * experts)
 
-    def ret_copy(s, j, i):
-        to = dev((ox if j else x), (oy if s else y), (z + nz - i) % nz, c)
-        slot = (s * 2 + j) * nz + i
-        return remote(ret_out.at[s, spot(ox if j else x, i), :], ret_in.at[slot], ret_sem, slot, to)
+    def ret_copy(s, e, i):
+        to = dev(x, (oy if s else y), (z + nz - i) % nz, c)
+        slot = (s * 2 + e) * nz + i
+        return remote(ret_out.at[s, e, pair(i), :], ret_in.at[slot], ret_sem, slot, to)
 
     def back(s):
         weight = jnp.sum(jnp.where(wanted, xm[s, :, half:].astype(f32), f32(0.0)), axis=1, keepdims=True)
         hid_copy[s].wait_recv()
 
-        def quarter_of(which):
-            cols = pl.ds(pl.multiple_of(which * quarter, quarter), quarter)
+        def piece_of(which, e):
+            cols = pl.ds(pl.multiple_of(which * quarter + e * piece, piece), piece)
             return (dot32(hid_out[s], wd[0, :, cols]) + dot32(hid_in[s], wd[1, :, cols])) * weight
 
-        part_out[s] = quarter_of(oc).astype(bf16)
-        go(part_copy[s])
-        own = quarter_of(c)
-        part_copy[s].wait_recv()
-        ret_out[s] = (own + part_in[s].astype(f32)).astype(bf16)
-        for i in (2, 1, 3, 0) if nz == 4 else range(nz):
-            for j in (1, 0):
-                if s or j or i:
-                    go(ret_copy(s, j, i))
+        for e in range(2):
+            part_out[s, e] = piece_of(oc, e).astype(bf16)
+            go(part_copy[s][e])
+        for e in range(2):
+            own = piece_of(c, e)
+            part_copy[s][e].wait_recv()
+            ret_out[s, e] = (own + part_in[s, e].astype(f32)).astype(bf16)
+            for i in (2, 1, 3, 0) if nz == 4 else range(nz):
+                if s or i:
+                    go(ret_copy(s, e, i))
 
     back(0)
     back(1)
 
-    sums = [jnp.zeros((block, quarter), f32), jnp.zeros((block, quarter), f32)]
-    sums[0] += ret_out[0, spot(x, 0), :].astype(f32)
-    for s in range(2):
-        for i in range(nz):
-            for j in range(2):
-                if s or j or i:
-                    ret_copy(s, j, i).wait_recv()
-                    sums[j] += ret_in[(s * 2 + j) * nz + i].astype(f32)
-    for j in range(2):
-        fin_out[:, j * quarter : (j + 1) * quarter] = jnp.where(first, sums[j][rows:], sums[j][:rows])
-    fin = go(remote(fin_out, fin_in, fin_sem, 0, sibling))
-    mine = [jnp.where(first, sums[j][:rows], sums[j][rows:]) for j in range(2)]
-    fin.wait_recv()
-    other = [fin_in[:, j * quarter : (j + 1) * quarter] for j in range(2)]
+    for e in range(2):
+        total = ret_out[0, e, pair(0), :].astype(f32)
+        for s in range(2):
+            for i in range(nz):
+                if s or i:
+                    ret_copy(s, e, i).wait_recv()
+                    total += ret_in[(s * 2 + e) * nz + i].astype(f32)
+        fin_out[:, e * piece : (e + 1) * piece] = total
+
+    def rows_of(xx, cc):
+        return pl.ds(pl.multiple_of((xx * 2 + cc) * rows, rows), rows)
+
+    fin_copy = [
+        remote(fin_out.at[rows_of(xx, cc), :], fin_in.at[n], fin_sem, n, to)
+        for n, (xx, cc, to) in enumerate(((ox, c, x_peer), (ox, oc, x_sibling), (x, oc, sibling)))
+    ]
+    for copy in fin_copy:
+        go(copy)
+    kept = fin_out[rows_of(x, c), :]
+    for copy in fin_copy:
+        copy.wait_recv()
     pieces = []
     for h in range(2):
         for q in range(2):
-            near = jnp.where(c == q, mine[0], other[0])
-            far = jnp.where(c == q, mine[1], other[1])
+            near = jnp.where(c == q, kept, fin_in[2])
+            far = jnp.where(c == q, fin_in[0], fin_in[1])
             pieces.append(jnp.where(x == h, near, far))
-    mixed = tok_ref[...].astype(f32) + jnp.concatenate(pieces, axis=1)
+    mixed = tok + jnp.concatenate(pieces, axis=1)
     factor = lax.rsqrt(jnp.mean(mixed * mixed, axis=1, keepdims=True) + 1e-06)
     out_ref[...] = (mixed * factor * gain_ref[...]).astype(bf16)
     for copy in sends:
@@ -254,13 +271,16 @@
     def sems(count):
         return pltpu.SemaphoreType.DMA((2, count))
 
-    whole = pl.BlockSpec(memory_space=pltpu.VMEM)
     return pl.pallas_call(
         functools.partial(fused_kernel, nz, experts),
         out_shape=jax.ShapeDtypeStruct((rows, width), bf16),
-        in_specs=[whole] * 4 + [pl.BlockSpec(memory_space=pl.ANY)] * 3,
-        out_specs=whole,
+        in_specs=[pl.BlockSpec(memory_space=pltpu.HBM)] * 7,
+        out_specs=pl.BlockSpec(memory_space=pltpu.VMEM),
         scratch_shapes=[
+            vmem((rows, width), bf16),
+            vmem(expert_ids.shape, jnp.int32),
+            vmem(gate_weights.shape, f32),
+            vmem((1, width), f32),
             vmem((2, half, ff_half), bf16),
             vmem((2, half, ff_half), bf16),
             vmem((2, ff_half, out_cols), bf16),
@@ -270,18 +290,19 @@
             vmem((2, stage, wide), bf16),
             vmem((2, stage, ff_half), bf16),
             vmem((2, stage, ff_half), bf16),
-            vmem((2, stage, quarter), bf16),
-            vmem((2, stage, quarter), bf16),
-            vmem((2, stage, quarter), bf16),
-            vmem((4 * nz, block, quarter), bf16),
-            vmem((rows, half), f32),
-            vmem((rows, half), f32),
+            vmem((2, 2, stage, quarter // 2), bf16),
+            vmem((2, 2, stage, quarter // 2), bf16),
+            vmem((2, 2, stage, quarter // 2), bf16),
+            vmem((4 * nz, 2 * block, quarter // 2), bf16),
+            vmem((2 * block, quarter), f32),
+            vmem((3, rows, quarter), f32),
+            pltpu.SemaphoreType.DMA((4,)),
             pltpu.SemaphoreType.DMA((6,)),
-            sems(1), sems(nz), sems(nz), sems(nz), sems(nz), sems(nz), sems(4), sems(2), sems(2),
-            sems(4 * nz), sems(1),
+            sems(1), sems(nz), sems(nz), sems(nz), sems(nz), sems(nz), sems(2 * nz), sems(2), sems(4),
+            sems(4 * nz), sems(3),
         ],
         compiler_params=pltpu.CompilerParams(
-            collective_id=0, has_side_effects=True, vmem_limit_bytes=48 * 1024 * 1024
+            collective_id=0, has_side_effects=True, vmem_limit_bytes=56 * 1024 * 1024
         ),
     )(tokens, expert_ids, gate_weights, norm_gain.reshape(1, width), w_gate, w_up, w_down)
 

time: 50.7 us -> 48.3 us (0.953)
  local copies, waits for them, and re-layouts: 5.75 us -> 1.47 us
  Pallas kernels: 44.6 us -> 46.6 us
    unnamed x11 -> x1, local copies, waits for them, and re-layouts: 5.75 us -> 1.47 us
    pallas_call x1, Pallas kernels: 44.6 us -> 46.6 us  [fused(): pl.pallas_call(functools.partial(fused_kernel, nz, experts), out_shape=ja...]
where the time goes in v2:
time: 48.3 us; the launch traced here: 48.1 us
  Pallas kernels  46.6 us (96%)
  local copies, waits for them, and re-layouts  1.47 us (3%)
    pallas_call x1, Pallas kernels, fused(): pl.pallas_call(functools.partial(fused_kernel, nz, experts), out_shape=ja...  46.6 us
    unnamed x1, local copies, waits for them, and re-layouts  1.47 us

profile of v2, /device:TPU:0, one launch (start us, length us, event | category | flops | bytes accessed | tf_op | source)
XLA Modules:
  0.0 48.1 jit_solution(1419588784911121904)
XLA Ops:
  0.0 46.6 %shard_map.73 = bf16[8,4096]{1,0:T(8,128)(2,1)} custom-call(bf16[8,4096]{1,0:T(8,128)(2,1)} %tok_hbm.1, s32[8,8]{1,0:T(8,128)} %ids_hbm.1, f32[8,8]{1,0:T(8,128)} %gates_hbm.1, f32[1,4096]{1,0:T(1,128)} %bitcast.1, bf16[1,4096,512]{2,1,0:T(8,128)(2,1)} %wg_hbm.1, bf16[1,4096,512]{2,1,0:T(8,128)(2,1)} %wu_hbm.1, bf16[1,1024,2048]{2,1,0:T(8,128)(2,1)} %wd_hbm.1), custom_call_target="tpu_custom_call" | custom-call | tf_op jit(solution)/shard_map/pallas_call | solution.py:274
  46.6 1.5 %copy.9 = bf16[8,4096]{1,0:T(8,128)(2,1)} copy(bf16[8,4096]{1,0:T(8,128)(2,1)} %shard_map.73) | data formatting | bytes 131072

commit v3 on v2

--- a/solution.py
+++ b/solution.py
@@ -29,6 +29,7 @@
     stage = 2 * nz * block
     piece = quarter // 2
     ff_half = wg.shape[2]
+    ff_part = ff_half // 2
     g, p = lax.axis_index("grp"), lax.axis_index("ep")
     y, x = g // 2, g % 2
     z, c = p // 2, p % 2
@@ -36,6 +37,9 @@
 
     def dev(xx, yy, zz, cc):
         return (yy * 2 + xx, zz * 2 + cc)
+
+    def along(i):
+        return (z // 2 * 2 + (z + i) % 2 + i // 2 * 2) % nz
 
     def remote(src, dst, sems, idx, to):
         return pltpu.make_async_remote_copy(
@@ -126,7 +130,7 @@
     xm[0, spot(x, 0), :] = jnp.concatenate([both(mine_half, theirs), coded], axis=1).astype(bf16)
 
     z_copy = [None] + [
-        remote(xm.at[0, spot(x, 0), :], xm.at[0, spot(x, i), :], z_sem, i, dev(x, y, (z + i) % nz, c))
+        remote(xm.at[0, spot(x, 0), :], xm.at[0, spot(x, i), :], z_sem, i, dev(x, y, along(i), c))
         for i in range(1, nz)
     ]
     x_copy = [remote(xm.at[0, spot(x, i), :], xm.at[0, spot(x, i), :], x_sem, i, x_peer) for i in range(nz)]
@@ -163,61 +167,68 @@
         if i not in by_y:
             go(d_copy[i])
 
+    def hid_copy(s, n):
+        return remote(hid_out.at[s, n], hid_in.at[s, n], hid_sem, 2 * s + n, x_peer)
+
     def front(s):
-        gate = dot32(xm[s, :, :half], wg[0])
-        up = dot32(xm[s, :, :half], wu[0])
-        if s == 0:
-            for load in loads[2:4]:
-                load.wait()
         for i in range(nz):
             sib_copy[s][i].wait_recv()
-        gate += dot32(xs[s, :, :half], wg[1])
-        up += dot32(xs[s, :, :half], wu[1])
-        hid_out[s] = (gate / (f32(1.0) + jnp.exp(-gate)) * up).astype(bf16)
-
-    hid_copy = [remote(hid_out.at[s], hid_in.at[s], hid_sem, s, x_peer) for s in range(2)]
-    for load in loads[:2]:
+
+        @pl.loop(0, 2)
+        def _(n):
+            cols = pl.ds(pl.multiple_of(n * ff_part, ff_part), ff_part)
+            gate = dot32(xm[s, :, :half], wg[0, :, cols]) + dot32(xs[s, :, :half], wg[1, :, cols])
+            up = dot32(xm[s, :, :half], wu[0, :, cols]) + dot32(xs[s, :, :half], wu[1, :, cols])
+            hid_out[s, n] = (gate / (f32(1.0) + jnp.exp(-gate)) * up).astype(bf16)
+            hid_copy(s, n).start()
+
+    for load in loads[:4]:
         load.wait()
     front(0)
-    go(hid_copy[0])
     for i in range(nz):
         d_land[i].wait_recv()
         go(sib_copy[1][i])
     front(1)
-    go(hid_copy[1])
 
     for load in loads[4:]:
         load.wait()
-    part_copy = [
-        [remote(part_out.at[s, e], part_in.at[s, e], part_sem, 2 * s + e, sibling) for e in range(2)]
-        for s in range(2)
-    ]
+    def part_copy(s, e):
+        return remote(part_out.at[s, e], part_in.at[s, e], part_sem, 2 * s + e, sibling)
+
     lanes = lax.broadcasted_iota(jnp.int32, (stage, LANES), 1)
     wanted = (lanes % experts == 2 * p + y) & (lanes < 3 * experts)
 
     def ret_copy(s, e, i):
-        to = dev(x, (oy if s else y), (z + nz - i) % nz, c)
+        to = dev(x, (oy if s else y), along(i), c)
         slot = (s * 2 + e) * nz + i
         return remote(ret_out.at[s, e, pair(i), :], ret_in.at[slot], ret_sem, slot, to)
 
     def back(s):
         weight = jnp.sum(jnp.where(wanted, xm[s, :, half:].astype(f32), f32(0.0)), axis=1, keepdims=True)
-        hid_copy[s].wait_recv()
+        for n in range(2):
+            hid_copy(s, n).wait_recv()
 
         def piece_of(which, e):
             cols = pl.ds(pl.multiple_of(which * quarter + e * piece, piece), piece)
-            return (dot32(hid_out[s], wd[0, :, cols]) + dot32(hid_in[s], wd[1, :, cols])) * weight
-
-        for e in range(2):
+            total = jnp.zeros((stage, piece), f32)
+            for n in range(2):
+                span = slice(n * ff_part, (n + 1) * ff_part)
+                total += dot32(hid_out[s, n], wd[0, span, cols]) + dot32(hid_in[s, n], wd[1, span, cols])
+            return total * weight
+
+        @pl.loop(0, 2)
+        def _(e):
             part_out[s, e] = piece_of(oc, e).astype(bf16)
-            go(part_copy[s][e])
-        for e in range(2):
+            part_copy(s, e).start()
+
+        @pl.loop(0, 2)
+        def _(e):
             own = piece_of(c, e)
-            part_copy[s][e].wait_recv()
+            part_copy(s, e).wait_recv()
             ret_out[s, e] = (own + part_in[s, e].astype(f32)).astype(bf16)
-            for i in (2, 1, 3, 0) if nz == 4 else range(nz):
+            for i in reversed(range(nz)):
                 if s or i:
-                    go(ret_copy(s, e, i))
+                    ret_copy(s, e, i).start()
 
     back(0)
     back(1)
@@ -252,6 +263,13 @@
     mixed = tok + jnp.concatenate(pieces, axis=1)
     factor = lax.rsqrt(jnp.mean(mixed * mixed, axis=1, keepdims=True) + 1e-06)
     out_ref[...] = (mixed * factor * gain_ref[...]).astype(bf16)
+    for s in range(2):
+        for e in range(2):
+            hid_copy(s, e).wait_send()
+            part_copy(s, e).wait_send()
+            for i in range(nz):
+                if s or i:
+                    ret_copy(s, e, i).wait_send()
     for copy in sends:
         copy.wait_send()
 
@@ -288,8 +306,8 @@
             vmem((rows, wide), f32),
             vmem((2, stage, wide), bf16),
             vmem((2, stage, wide), bf16),
-            vmem((2, stage, ff_half), bf16),
-            vmem((2, stage, ff_half), bf16),
+            vmem((2, 2, stage, ff_half // 2), bf16),
+            vmem((2, 2, stage, ff_half // 2), bf16),
             vmem((2, 2, stage, quarter // 2), bf16),
             vmem((2, 2, stage, quarter // 2), bf16),
             vmem((2, 2, stage, quarter // 2), bf16),
@@ -298,7 +316,7 @@
             vmem((3, rows, quarter), f32),
             pltpu.SemaphoreType.DMA((4,)),
             pltpu.SemaphoreType.DMA((6,)),
-            sems(1), sems(nz), sems(nz), sems(nz), sems(nz), sems(nz), sems(2 * nz), sems(2), sems(4),
+            sems(1), sems(nz), sems(nz), sems(nz), sems(nz), sems(nz), sems(2 * nz), sems(4), sems(4),
             sems(4 * nz), sems(3),
         ],
         compiler_params=pltpu.CompilerParams(
@@ -374,7 +392,7 @@
 
 def shards(tokens, *rest):
     all_rows = tokens.shape[0] * lax.axis_size("grp") * lax.axis_size("ep")
-    dense = lax.axis_size("grp") == 4 and lax.axis_size("ep") % 2 == 0 and all_rows <= 256
+    dense = lax.axis_size("grp") == 4 and lax.axis_size("ep") == 8 and all_rows <= 256
     return (fused if dense else routed)(tokens, *rest)
 
 

time: 48.3 us -> 47.6 us (0.986)
  Pallas kernels: 46.6 us -> 45.9 us
    pallas_call x1, Pallas kernels: 46.6 us -> 45.9 us  [fused(): pl.pallas_call(functools.partial(fused_kernel, nz, experts), out_shape=ja...]
where the time goes in v3:
time: 47.6 us; the launch traced here: 47.4 us
  Pallas kernels  45.9 us (96%)
  local copies, waits for them, and re-layouts  1.47 us (3%)
    pallas_call x1, Pallas kernels, fused(): pl.pallas_call(functools.partial(fused_kernel, nz, experts), out_shape=ja...  45.9 us
    unnamed x1, local copies, waits for them, and re-layouts  1.47 us

profile of v3, /device:TPU:0, one launch (start us, length us, event | category | flops | bytes accessed | tf_op | source)
XLA Modules:
  0.0 47.4 jit_solution(8484537061962051233)
XLA Ops:
  0.0 45.9 %shard_map.73 = bf16[8,4096]{1,0:T(8,128)(2,1)} custom-call(bf16[8,4096]{1,0:T(8,128)(2,1)} %tok_hbm.1, s32[8,8]{1,0:T(8,128)} %ids_hbm.1, f32[8,8]{1,0:T(8,128)} %gates_hbm.1, f32[1,4096]{1,0:T(1,128)} %bitcast.1, bf16[1,4096,512]{2,1,0:T(8,128)(2,1)} %wg_hbm.1, bf16[1,4096,512]{2,1,0:T(8,128)(2,1)} %wu_hbm.1, bf16[1,1024,2048]{2,1,0:T(8,128)(2,1)} %wd_hbm.1), custom_call_target="tpu_custom_call" | custom-call | tf_op jit(solution)/shard_map/pallas_call | solution.py:292
  45.9 1.5 %copy.9 = bf16[8,4096]{1,0:T(8,128)(2,1)} copy(bf16[8,4096]{1,0:T(8,128)(2,1)} %shard_map.73) | data formatting | bytes 131072

commit v4 on v3

--- a/solution.py
+++ b/solution.py
@@ -18,8 +18,8 @@
 def fused_kernel(
     nz, experts,
     tok_hbm, ids_hbm, gates_hbm, gain_hbm, wg_hbm, wu_hbm, wd_hbm, out_ref,
-    tok_ref, ids_ref, gates_ref, gain_ref, wg, wu, wd, s_out, s_in, xm, xs, hid_out, hid_in, part_out, part_in, ret_out, ret_in, fin_out, fin_in,
-    t_sem, w_sem, s_sem, z_sem, x_sem, y_sem, dx_sem, dy_sem, sib_sem, hid_sem, part_sem, ret_sem, fin_sem,
+    tok_ref, ids_ref, gates_ref, gain_ref, wg, wu, wd, xb, lhs, tabs, hid_out, hid_in, part_out, part_in, ret_out, ret_in, fin_out, fin_in,
+    t_sem, w_sem, z_sem, x_sem, y_sem, dx_sem, dy_sem, sib_sem, hid_sem, part_sem, ret_sem, fin_sem,
 ):
     f32, bf16 = jnp.float32, jnp.bfloat16
     rows, width = tok_ref.shape
@@ -63,10 +63,9 @@
 
     loads = []
     n = 0
-    for mine, at_k in ((0, c), (1, oc)):
+    for k in range(2):
         for src, dst in ((wg_hbm, wg), (wu_hbm, wu)):
-            span = pl.ds(pl.multiple_of(at_k * half, half), half)
-            loads.append(pltpu.make_async_copy(src.at[0, span, :], dst.at[mine], w_sem.at[n]))
+            loads.append(pltpu.make_async_copy(src.at[0, pl.ds(k * half, half), :], dst.at[k], w_sem.at[n]))
             n += 1
     for mine, at_k in ((0, x), (1, ox)):
         span = pl.ds(pl.multiple_of(at_k * ff_half, ff_half), ff_half)
@@ -90,32 +89,11 @@
     for k in range(ids_ref.shape[1]):
         table += jnp.where(ids_ref[:, k : k + 1] == lane % experts, gates_ref[:, k : k + 1], f32(0.0))
     tok = tok_ref[...].astype(f32)
-    first = c == 0
-    mine_half = jnp.where(first, tok[:, :half], tok[:, half:])
-    s_out[:, :half] = jnp.where(first, tok[:, half:], tok[:, :half])
-    s_out[:, half:] = table
-    pl.semaphore_wait(barrier, greeted)
-
-    sends = []
-
-    def go(copy):
-        copy.start()
-        sends.append(copy)
-        return copy
-
-    swap = go(remote(s_out, s_in, s_sem, 0, sibling))
-    swap.wait_recv()
-    theirs, their_table = s_in[:, :half], s_in[:, half:]
-
-    def both(a, b):
-        return jnp.where(first, jnp.concatenate([a, b], axis=0), jnp.concatenate([b, a], axis=0))
-
-    pair_table = both(table, their_table)
-    high = pair_table.astype(bf16)
-    rest = pair_table - high.astype(f32)
+    high = table.astype(bf16)
+    rest = table - high.astype(f32)
     middle = rest.astype(bf16)
     low = (rest - middle.astype(f32)).astype(bf16)
-    part = lax.broadcasted_iota(jnp.int32, (block, LANES), 1) // experts
+    part = lane // experts
     coded = jnp.where(
         part == 0, high.astype(f32),
         jnp.where(part == 1, middle.astype(f32), jnp.where(part == 2, low.astype(f32), f32(0.0))),
@@ -127,28 +105,55 @@
     def pair(i):
         return slice(2 * i * block, 2 * (i + 1) * block)
 
-    xm[0, spot(x, 0), :] = jnp.concatenate([both(mine_half, theirs), coded], axis=1).astype(bf16)
+    xb[c, 0, spot(x, 0), :] = jnp.concatenate(
+        [
+            jnp.concatenate([tok[:, :half], coded], axis=1),
+            jnp.concatenate([tok[:, half:], jnp.zeros_like(coded)], axis=1),
+        ],
+        axis=0,
+    ).astype(bf16)
+
+    pl.semaphore_wait(barrier, greeted)
+    sends = []
+
+    def go(copy):
+        copy.start()
+        sends.append(copy)
 
     z_copy = [None] + [
-        remote(xm.at[0, spot(x, 0), :], xm.at[0, spot(x, i), :], z_sem, i, dev(x, y, along(i), c))
+        remote(xb.at[c, 0, spot(x, 0), :], xb.at[c, 0, spot(x, i), :], z_sem, i, dev(x, y, along(i), c))
         for i in range(1, nz)
     ]
-    x_copy = [remote(xm.at[0, spot(x, i), :], xm.at[0, spot(x, i), :], x_sem, i, x_peer) for i in range(nz)]
-    x_land = [remote(xm.at[0, spot(ox, i), :], xm.at[0, spot(ox, i), :], x_sem, i, x_peer) for i in range(nz)]
-    y_copy = [remote(xm.at[0, spot(x, i), :], xm.at[1, spot(x, i), :], y_sem, i, y_peer) for i in range(nz)]
+    x_copy = [remote(xb.at[c, 0, spot(x, i), :], xb.at[c, 0, spot(x, i), :], x_sem, i, x_peer) for i in range(nz)]
+    x_land = [remote(xb.at[c, 0, spot(ox, i), :], xb.at[c, 0, spot(ox, i), :], x_sem, i, x_peer) for i in range(nz)]
+    y_copy = [remote(xb.at[c, 0, spot(x, i), :], xb.at[c, 1, spot(x, i), :], y_sem, i, y_peer) for i in range(nz)]
     by_y = [i for i in range(nz) if i % 4 in (1, 2)]
     d_copy, d_land = [], []
     for i in range(nz):
         if i in by_y:
-            d_copy.append(remote(xm.at[0, spot(ox, i), :], xm.at[1, spot(ox, i), :], dy_sem, i, y_peer))
+            d_copy.append(remote(xb.at[c, 0, spot(ox, i), :], xb.at[c, 1, spot(ox, i), :], dy_sem, i, y_peer))
             d_land.append(d_copy[-1])
         else:
-            d_copy.append(remote(xm.at[1, spot(x, i), :], xm.at[1, spot(x, i), :], dx_sem, i, x_peer))
-            d_land.append(remote(xm.at[1, spot(ox, i), :], xm.at[1, spot(ox, i), :], dx_sem, i, x_peer))
-    sib_copy = [
-        [remote(xm.at[s, pair(i), :], xs.at[s, pair(i), :], sib_sem, s * nz + i, sibling) for i in range(nz)]
-        for s in range(2)
+            d_copy.append(remote(xb.at[c, 1, spot(x, i), :], xb.at[c, 1, spot(x, i), :], dx_sem, i, x_peer))
+            d_land.append(remote(xb.at[c, 1, spot(ox, i), :], xb.at[c, 1, spot(ox, i), :], dx_sem, i, x_peer))
+    sib_copy, sib_land = [
+        [
+            [remote(xb.at[k, s, pair(i), :], xb.at[k, s, pair(i), :], sib_sem, s * nz + i, sibling) for i in range(nz)]
+            for s in range(2)
+        ]
+        for k in (c, oc)
     ]
+
+    def assemble(s, i):
+        sib_land[s][i].wait_recv()
+        for b in (2 * i, 2 * i + 1):
+            at = slice(b * block, (b + 1) * block)
+            two = [xb[k, s, at, :].astype(f32) for k in range(2)]
+            for h in range(2):
+                lhs[s, h, at, :] = jnp.concatenate(
+                    [v[h * rows : (h + 1) * rows, :half] for v in two], axis=0
+                ).astype(bf16)
+            tabs[s, at, :] = jnp.concatenate([v[:rows, half:] for v in two], axis=0)
 
     for i in range(1, nz):
         go(z_copy[i])
@@ -166,19 +171,19 @@
         y_copy[i].wait_recv()
         if i not in by_y:
             go(d_copy[i])
+        if i:
+            assemble(0, i - 1)
+    assemble(0, nz - 1)
 
     def hid_copy(s, n):
         return remote(hid_out.at[s, n], hid_in.at[s, n], hid_sem, 2 * s + n, x_peer)
 
     def front(s):
-        for i in range(nz):
-            sib_copy[s][i].wait_recv()
-
         @pl.loop(0, 2)
         def _(n):
             cols = pl.ds(pl.multiple_of(n * ff_part, ff_part), ff_part)
-            gate = dot32(xm[s, :, :half], wg[0, :, cols]) + dot32(xs[s, :, :half], wg[1, :, cols])
-            up = dot32(xm[s, :, :half], wu[0, :, cols]) + dot32(xs[s, :, :half], wu[1, :, cols])
+            gate = dot32(lhs[s, 0], wg[0, :, cols]) + dot32(lhs[s, 1], wg[1, :, cols])
+            up = dot32(lhs[s, 0], wu[0, :, cols]) + dot32(lhs[s, 1], wu[1, :, cols])
             hid_out[s, n] = (gate / (f32(1.0) + jnp.exp(-gate)) * up).astype(bf16)
             hid_copy(s, n).start()
 
@@ -188,6 +193,9 @@
     for i in range(nz):
         d_land[i].wait_recv()
         go(sib_copy[1][i])
+        if i:
+            assemble(1, i - 1)
+    assemble(1, nz - 1)
     front(1)
 
     for load in loads[4:]:
@@ -204,7 +212,7 @@
         return remote(ret_out.at[s, e, pair(i), :], ret_in.at[slot], ret_sem, slot, to)
 
     def back(s):
-        weight = jnp.sum(jnp.where(wanted, xm[s, :, half:].astype(f32), f32(0.0)), axis=1, keepdims=True)
+        weight = jnp.sum(jnp.where(wanted, tabs[s], f32(0.0)), axis=1, keepdims=True)
         for n in range(2):
             hid_copy(s, n).wait_recv()
 
@@ -302,10 +310,9 @@
             vmem((2, half, ff_half), bf16),
             vmem((2, half, ff_half), bf16),
             vmem((2, ff_half, out_cols), bf16),
-            vmem((rows, wide), f32),
-            vmem((rows, wide), f32),
-            vmem((2, stage, wide), bf16),
-            vmem((2, stage, wide), bf16),
+            vmem((2, 2, stage, wide), bf16),
+            vmem((2, 2, stage, half), bf16),
+            vmem((2, stage, LANES), f32),
             vmem((2, 2, stage, ff_half // 2), bf16),
             vmem((2, 2, stage, ff_half // 2), bf16),
             vmem((2, 2, stage, quarter // 2), bf16),
@@ -316,7 +323,7 @@
             vmem((3, rows, quarter), f32),
             pltpu.SemaphoreType.DMA((4,)),
             pltpu.SemaphoreType.DMA((6,)),
-            sems(1), sems(nz), sems(nz), sems(nz), sems(nz), sems(nz), sems(2 * nz), sems(4), sems(4),
+            sems(nz), sems(nz), sems(nz), sems(nz), sems(nz), sems(2 * nz), sems(4), sems(4),
             sems(4 * nz), sems(3),
         ],
         compiler_params=pltpu.CompilerParams(

time: 47.6 us -> 45.7 us (0.960)
  Pallas kernels: 45.9 us -> 44.1 us
    pallas_call x1, Pallas kernels: 45.9 us -> 44.1 us  [fused(): pl.pallas_call(functools.partial(fused_kernel, nz, experts), out_shape=ja...]
where the time goes in v4:
time: 45.7 us; the launch traced here: 45.5 us
  Pallas kernels  44.1 us (96%)
  local copies, waits for them, and re-layouts  1.47 us (3%)
    pallas_call x1, Pallas kernels, fused(): pl.pallas_call(functools.partial(fused_kernel, nz, experts), out_shape=ja...  44.1 us
    unnamed x1, local copies, waits for them, and re-layouts  1.47 us

profile of v4, /device:TPU:0, one launch (start us, length us, event | category | flops | bytes accessed | tf_op | source)
XLA Modules:
  0.0 45.5 jit_solution(14961666658343152038)
XLA Ops:
  0.0 44.1 %shard_map.73 = bf16[8,4096]{1,0:T(8,128)(2,1)} custom-call(bf16[8,4096]{1,0:T(8,128)(2,1)} %tok_hbm.1, s32[8,8]{1,0:T(8,128)} %ids_hbm.1, f32[8,8]{1,0:T(8,128)} %gates_hbm.1, f32[1,4096]{1,0:T(1,128)} %bitcast.1, bf16[1,4096,512]{2,1,0:T(8,128)(2,1)} %wg_hbm.1, bf16[1,4096,512]{2,1,0:T(8,128)(2,1)} %wu_hbm.1, bf16[1,1024,2048]{2,1,0:T(8,128)(2,1)} %wd_hbm.1), custom_call_target="tpu_custom_call" | custom-call | tf_op jit(solution)/shard_map/pallas_call | solution.py:300
  44.1 1.5 %copy.9 = bf16[8,4096]{1,0:T(8,128)(2,1)} copy(bf16[8,4096]{1,0:T(8,128)(2,1)} %shard_map.73) | data formatting | bytes 131072

commit v5 on v4

--- a/solution.py
+++ b/solution.py
@@ -159,11 +159,12 @@
         go(z_copy[i])
     go(x_copy[0])
     go(y_copy[0])
-    for i in range(nz):
-        if i + 1 < nz:
-            z_copy[i + 1].wait_recv()
-            go(x_copy[i + 1])
-            go(y_copy[i + 1])
+    def onward(i):
+        z_copy[i].wait_recv()
+        go(x_copy[i])
+        go(y_copy[i])
+
+    def arrive(i):
         x_land[i].wait_recv()
         if i in by_y:
             go(d_copy[i])
@@ -171,39 +172,45 @@
         y_copy[i].wait_recv()
         if i not in by_y:
             go(d_copy[i])
-        if i:
-            assemble(0, i - 1)
-    assemble(0, nz - 1)
-
-    def hid_copy(s, n):
-        return remote(hid_out.at[s, n], hid_in.at[s, n], hid_sem, 2 * s + n, x_peer)
-
-    def front(s):
+
+    def arrive_far(i):
+        d_land[i].wait_recv()
+        go(sib_copy[1][i])
+
+    mid = nz // 2
+    chunks = [(0, 0, range(0, mid)), (1, 0, range(mid, nz)), (2, 1, range(0, mid)), (3, 1, range(mid, nz))]
+
+    def rows_in(pairs):
+        return slice(2 * pairs[0] * block, 2 * (pairs[-1] + 1) * block)
+
+    def hid_copy(chunk, n):
+        number, s, pairs = chunk
+        at = rows_in(pairs)
+        return remote(hid_out.at[s, n, at], hid_in.at[s, n, at], hid_sem, 2 * number + n, x_peer)
+
+    def front(chunk):
+        number, s, pairs = chunk
+        at = rows_in(pairs)
+        for i in pairs:
+            assemble(s, i)
+        if number == 0:
+            for load in loads[:4]:
+                load.wait()
+
         @pl.loop(0, 2)
         def _(n):
             cols = pl.ds(pl.multiple_of(n * ff_part, ff_part), ff_part)
-            gate = dot32(lhs[s, 0], wg[0, :, cols]) + dot32(lhs[s, 1], wg[1, :, cols])
-            up = dot32(lhs[s, 0], wu[0, :, cols]) + dot32(lhs[s, 1], wu[1, :, cols])
-            hid_out[s, n] = (gate / (f32(1.0) + jnp.exp(-gate)) * up).astype(bf16)
-            hid_copy(s, n).start()
-
-    for load in loads[:4]:
-        load.wait()
-    front(0)
-    for i in range(nz):
-        d_land[i].wait_recv()
-        go(sib_copy[1][i])
-        if i:
-            assemble(1, i - 1)
-    assemble(1, nz - 1)
-    front(1)
-
-    for load in loads[4:]:
-        load.wait()
-    def part_copy(s, e):
-        return remote(part_out.at[s, e], part_in.at[s, e], part_sem, 2 * s + e, sibling)
-
-    lanes = lax.broadcasted_iota(jnp.int32, (stage, LANES), 1)
+            gate = dot32(lhs[s, 0, at], wg[0, :, cols]) + dot32(lhs[s, 1, at], wg[1, :, cols])
+            up = dot32(lhs[s, 0, at], wu[0, :, cols]) + dot32(lhs[s, 1, at], wu[1, :, cols])
+            hid_out[s, n, at] = (gate / (f32(1.0) + jnp.exp(-gate)) * up).astype(bf16)
+            hid_copy(chunk, n).start()
+
+    def part_copy(chunk, e):
+        number, s, pairs = chunk
+        at = rows_in(pairs)
+        return remote(part_out.at[s, e, at], part_in.at[s, e, at], part_sem, 2 * number + e, sibling)
+
+    lanes = lax.broadcasted_iota(jnp.int32, (stage // 2, LANES), 1)
     wanted = (lanes % experts == 2 * p + y) & (lanes < 3 * experts)
 
     def ret_copy(s, e, i):
@@ -211,35 +218,68 @@
         slot = (s * 2 + e) * nz + i
         return remote(ret_out.at[s, e, pair(i), :], ret_in.at[slot], ret_sem, slot, to)
 
-    def back(s):
-        weight = jnp.sum(jnp.where(wanted, tabs[s], f32(0.0)), axis=1, keepdims=True)
+    def piece_of(chunk, which, e):
+        number, s, pairs = chunk
+        at = rows_in(pairs)
+        cols = pl.ds(pl.multiple_of(which * quarter + e * piece, piece), piece)
+        total = jnp.zeros((len(pairs) * 2 * block, piece), f32)
         for n in range(2):
-            hid_copy(s, n).wait_recv()
-
-        def piece_of(which, e):
-            cols = pl.ds(pl.multiple_of(which * quarter + e * piece, piece), piece)
-            total = jnp.zeros((stage, piece), f32)
-            for n in range(2):
-                span = slice(n * ff_part, (n + 1) * ff_part)
-                total += dot32(hid_out[s, n], wd[0, span, cols]) + dot32(hid_in[s, n], wd[1, span, cols])
-            return total * weight
+            span = slice(n * ff_part, (n + 1) * ff_part)
+            total += dot32(hid_out[s, n, at], wd[0, span, cols]) + dot32(hid_in[s, n, at], wd[1, span, cols])
+        weight = jnp.sum(jnp.where(wanted, tabs[s, at], f32(0.0)), axis=1, keepdims=True)
+        return total * weight
+
+    def back_theirs(chunk):
+        number, s, pairs = chunk
+        at = rows_in(pairs)
+        if number == 0:
+            for load in loads[4:]:
+                load.wait()
+        for n in range(2):
+            hid_copy(chunk, n).wait_recv()
 
         @pl.loop(0, 2)
         def _(e):
-            part_out[s, e] = piece_of(oc, e).astype(bf16)
-            part_copy(s, e).start()
+            part_out[s, e, at] = piece_of(chunk, oc, e).astype(bf16)
+            part_copy(chunk, e).start()
+
+    def back_mine(chunk):
+        number, s, pairs = chunk
+        at = rows_in(pairs)
 
         @pl.loop(0, 2)
         def _(e):
-            own = piece_of(c, e)
-            part_copy(s, e).wait_recv()
-            ret_out[s, e] = (own + part_in[s, e].astype(f32)).astype(bf16)
-            for i in reversed(range(nz)):
+            own = piece_of(chunk, c, e)
+            part_copy(chunk, e).wait_recv()
+            ret_out[s, e, at] = (own + part_in[s, e, at].astype(f32)).astype(bf16)
+            for i in reversed(pairs):
                 if s or i:
                     ret_copy(s, e, i).start()
 
-    back(0)
-    back(1)
+    onward(1)
+    arrive(0)
+    for i in range(2, nz):
+        onward(i)
+    for i in range(1, mid):
+        arrive(i)
+    front(chunks[0])
+    for i in range(mid):
+        arrive_far(i)
+    for i in range(mid, nz):
+        arrive(i)
+    front(chunks[1])
+    for i in range(mid, nz):
+        arrive_far(i)
+    front(chunks[2])
+    back_theirs(chunks[0])
+    front(chunks[3])
+    back_mine(chunks[0])
+    back_theirs(chunks[1])
+    back_theirs(chunks[2])
+    back_mine(chunks[1])
+    back_mine(chunks[2])
+    back_theirs(chunks[3])
+    back_mine(chunks[3])
 
     for e in range(2):
         total = ret_out[0, e, pair(0), :].astype(f32)
@@ -271,11 +311,12 @@
     mixed = tok + jnp.concatenate(pieces, axis=1)
     factor = lax.rsqrt(jnp.mean(mixed * mixed, axis=1, keepdims=True) + 1e-06)
     out_ref[...] = (mixed * factor * gain_ref[...]).astype(bf16)
-    for s in range(2):
+    for chunk in chunks:
+        s, pairs = chunk[1:]
         for e in range(2):
-            hid_copy(s, e).wait_send()
-            part_copy(s, e).wait_send()
-            for i in range(nz):
+            hid_copy(chunk, e).wait_send()
+            part_copy(chunk, e).wait_send()
+            for i in pairs:
                 if s or i:
                     ret_copy(s, e, i).wait_send()
     for copy in sends:
@@ -323,7 +364,7 @@
             vmem((3, rows, quarter), f32),
             pltpu.SemaphoreType.DMA((4,)),
             pltpu.SemaphoreType.DMA((6,)),
-            sems(nz), sems(nz), sems(nz), sems(nz), sems(nz), sems(2 * nz), sems(4), sems(4),
+            sems(nz), sems(nz), sems(nz), sems(nz), sems(nz), sems(2 * nz), sems(8), sems(8),
             sems(4 * nz), sems(3),
         ],
         compiler_params=pltpu.CompilerParams(

time: 45.7 us -> 48 us (1.050)
  Pallas kernels: 44.1 us -> 46.3 us
    pallas_call x1, Pallas kernels: 44.1 us -> 46.3 us  [fused(): pl.pallas_call(functools.partial(fused_kernel, nz, experts), out_shape=ja...]
where the time goes in v5:
time: 48 us; the launch traced here: 47.8 us
  Pallas kernels  46.3 us (96%)
  local copies, waits for them, and re-layouts  1.47 us (3%)
    pallas_call x1, Pallas kernels, fused(): pl.pallas_call(functools.partial(fused_kernel, nz, experts), out_shape=ja...  46.3 us
    unnamed x1, local copies, waits for them, and re-layouts  1.47 us

profile of v5, /device:TPU:0, one launch (start us, length us, event | category | flops | bytes accessed | tf_op | source)
XLA Modules:
  0.0 47.8 jit_solution(5953626224939712879)
XLA Ops:
  0.0 46.3 %shard_map.73 = bf16[8,4096]{1,0:T(8,128)(2,1)} custom-call(bf16[8,4096]{1,0:T(8,128)(2,1)} %tok_hbm.1, s32[8,8]{1,0:T(8,128)} %ids_hbm.1, f32[8,8]{1,0:T(8,128)} %gates_hbm.1, f32[1,4096]{1,0:T(1,128)} %bitcast.1, bf16[1,4096,512]{2,1,0:T(8,128)(2,1)} %wg_hbm.1, bf16[1,4096,512]{2,1,0:T(8,128)(2,1)} %wu_hbm.1, bf16[1,1024,2048]{2,1,0:T(8,128)(2,1)} %wd_hbm.1), custom_call_target="tpu_custom_call" | custom-call | tf_op jit(solution)/shard_map/pallas_call | solution.py:341
  46.3 1.5 %copy.9 = bf16[8,4096]{1,0:T(8,128)(2,1)} copy(bf16[8,4096]{1,0:T(8,128)(2,1)} %shard_map.73) | data formatting | bytes 131072

commit v6 on v5

--- a/solution.py
+++ b/solution.py
@@ -18,7 +18,7 @@
 def fused_kernel(
     nz, experts,
     tok_hbm, ids_hbm, gates_hbm, gain_hbm, wg_hbm, wu_hbm, wd_hbm, out_ref,
-    tok_ref, ids_ref, gates_ref, gain_ref, wg, wu, wd, xb, lhs, tabs, hid_out, hid_in, part_out, part_in, ret_out, ret_in, fin_out, fin_in,
+    tok_ref, ids_ref, gates_ref, gain_ref, wgu, wd, xb, lhs, tabs, hid, part_out, part_in, ret_out, ret_in, fin_out, fin_in,
     t_sem, w_sem, z_sem, x_sem, y_sem, dx_sem, dy_sem, sib_sem, hid_sem, part_sem, ret_sem, fin_sem,
 ):
     f32, bf16 = jnp.float32, jnp.bfloat16
@@ -28,8 +28,8 @@
     block = 2 * rows
     stage = 2 * nz * block
     piece = quarter // 2
-    ff_half = wg.shape[2]
-    ff_part = ff_half // 2
+    ff_part = wgu.shape[2] // 2
+    ff_half = 2 * ff_part
     g, p = lax.axis_index("grp"), lax.axis_index("ep")
     y, x = g // 2, g % 2
     z, c = p // 2, p % 2
@@ -62,15 +62,22 @@
         load.start()
 
     loads = []
-    n = 0
-    for k in range(2):
-        for src, dst in ((wg_hbm, wg), (wu_hbm, wu)):
-            loads.append(pltpu.make_async_copy(src.at[0, pl.ds(k * half, half), :], dst.at[k], w_sem.at[n]))
-            n += 1
+    for n in range(2):
+        for k, src in enumerate((wg_hbm, wu_hbm)):
+            from_cols, to_cols = pl.ds(n * ff_part, ff_part), pl.ds(k * ff_part, ff_part)
+            loads.append(
+                pltpu.make_async_copy(src.at[0, :, from_cols], wgu.at[n, :, to_cols], w_sem.at[len(loads)])
+            )
     for mine, at_k in ((0, x), (1, ox)):
         span = pl.ds(pl.multiple_of(at_k * ff_half, ff_half), ff_half)
-        loads.append(pltpu.make_async_copy(wd_hbm.at[0, span, :], wd.at[mine], w_sem.at[n]))
-        n += 1
+        for e in range(4):
+            loads.append(
+                pltpu.make_async_copy(
+                    wd_hbm.at[0, span, pl.ds(e * piece, piece)],
+                    wd.at[e, pl.ds(mine * ff_half, ff_half), :],
+                    w_sem.at[len(loads)],
+                )
+            )
 
     barrier = pltpu.get_barrier_semaphore()
     greeted = 0
@@ -150,7 +157,7 @@
             at = slice(b * block, (b + 1) * block)
             two = [xb[k, s, at, :].astype(f32) for k in range(2)]
             for h in range(2):
-                lhs[s, h, at, :] = jnp.concatenate(
+                lhs[s, at, h * half : (h + 1) * half] = jnp.concatenate(
                     [v[h * rows : (h + 1) * rows, :half] for v in two], axis=0
                 ).astype(bf16)
             tabs[s, at, :] = jnp.concatenate([v[:rows, half:] for v in two], axis=0)
@@ -177,8 +184,7 @@
         d_land[i].wait_recv()
         go(sib_copy[1][i])
 
-    mid = nz // 2
-    chunks = [(0, 0, range(0, mid)), (1, 0, range(mid, nz)), (2, 1, range(0, mid)), (3, 1, range(mid, nz))]
+    chunks = [(0, 0, range(nz)), (1, 1, range(nz))]
 
     def rows_in(pairs):
         return slice(2 * pairs[0] * block, 2 * (pairs[-1] + 1) * block)
@@ -186,23 +192,21 @@
     def hid_copy(chunk, n):
         number, s, pairs = chunk
         at = rows_in(pairs)
-        return remote(hid_out.at[s, n, at], hid_in.at[s, n, at], hid_sem, 2 * number + n, x_peer)
+        return remote(hid.at[s, n, at], hid.at[s, 2 + n, at], hid_sem, 2 * number + n, x_peer)
 
     def front(chunk):
         number, s, pairs = chunk
         at = rows_in(pairs)
-        for i in pairs:
-            assemble(s, i)
+        assemble(s, pairs[-1])
         if number == 0:
             for load in loads[:4]:
                 load.wait()
 
         @pl.loop(0, 2)
         def _(n):
-            cols = pl.ds(pl.multiple_of(n * ff_part, ff_part), ff_part)
-            gate = dot32(lhs[s, 0, at], wg[0, :, cols]) + dot32(lhs[s, 1, at], wg[1, :, cols])
-            up = dot32(lhs[s, 0, at], wu[0, :, cols]) + dot32(lhs[s, 1, at], wu[1, :, cols])
-            hid_out[s, n, at] = (gate / (f32(1.0) + jnp.exp(-gate)) * up).astype(bf16)
+            both = dot32(lhs[s, at], wgu[n])
+            gate, up = both[:, :ff_part], both[:, ff_part:]
+            hid[s, n, at] = (gate / (f32(1.0) + jnp.exp(-gate)) * up).astype(bf16)
             hid_copy(chunk, n).start()
 
     def part_copy(chunk, e):
@@ -210,7 +214,7 @@
         at = rows_in(pairs)
         return remote(part_out.at[s, e, at], part_in.at[s, e, at], part_sem, 2 * number + e, sibling)
 
-    lanes = lax.broadcasted_iota(jnp.int32, (stage // 2, LANES), 1)
+    lanes = lax.broadcasted_iota(jnp.int32, (stage, LANES), 1)
     wanted = (lanes % experts == 2 * p + y) & (lanes < 3 * experts)
 
     def ret_copy(s, e, i):
@@ -221,11 +225,7 @@
     def piece_of(chunk, which, e):
         number, s, pairs = chunk
         at = rows_in(pairs)
-        cols = pl.ds(pl.multiple_of(which * quarter + e * piece, piece), piece)
-        total = jnp.zeros((len(pairs) * 2 * block, piece), f32)
-        for n in range(2):
-            span = slice(n * ff_part, (n + 1) * ff_part)
-            total += dot32(hid_out[s, n, at], wd[0, span, cols]) + dot32(hid_in[s, n, at], wd[1, span, cols])
+        total = dot32(jnp.concatenate([hid[s, n, at] for n in range(4)], axis=1), wd[which * 2 + e])
         weight = jnp.sum(jnp.where(wanted, tabs[s, at], f32(0.0)), axis=1, keepdims=True)
         return total * weight
 
@@ -256,30 +256,21 @@
                 if s or i:
                     ret_copy(s, e, i).start()
 
-    onward(1)
-    arrive(0)
-    for i in range(2, nz):
-        onward(i)
-    for i in range(1, mid):
+    for i in range(nz):
+        if i + 1 < nz:
+            onward(i + 1)
         arrive(i)
+        if i:
+            assemble(0, i - 1)
     front(chunks[0])
-    for i in range(mid):
+    for i in range(nz):
         arrive_far(i)
-    for i in range(mid, nz):
-        arrive(i)
+        if i:
+            assemble(1, i - 1)
     front(chunks[1])
-    for i in range(mid, nz):
-        arrive_far(i)
-    front(chunks[2])
-    back_theirs(chunks[0])
-    front(chunks[3])
-    back_mine(chunks[0])
-    back_theirs(chunks[1])
-    back_theirs(chunks[2])
-    back_mine(chunks[1])
-    back_mine(chunks[2])
-    back_theirs(chunks[3])
-    back_mine(chunks[3])
+    for chunk in chunks:
+        back_theirs(chunk)
+        back_mine(chunk)
 
     for e in range(2):
         total = ret_out[0, e, pair(0), :].astype(f32)
@@ -332,7 +323,7 @@
     block = 2 * rows
     stage = 2 * nz * block
     wide = half + LANES
-    ff_half, out_cols = w_gate.shape[2], w_down.shape[2]
+    ff_half = w_gate.shape[2]
     vmem = pltpu.VMEM
 
     def sems(count):
@@ -348,14 +339,12 @@
             vmem(expert_ids.shape, jnp.int32),
             vmem(gate_weights.shape, f32),
             vmem((1, width), f32),
-            vmem((2, half, ff_half), bf16),
-            vmem((2, half, ff_half), bf16),
-            vmem((2, ff_half, out_cols), bf16),
+            vmem((2, width, ff_half), bf16),
+            vmem((4, 2 * ff_half, quarter // 2), bf16),
             vmem((2, 2, stage, wide), bf16),
-            vmem((2, 2, stage, half), bf16),
+            vmem((2, stage, width), bf16),
             vmem((2, stage, LANES), f32),
-            vmem((2, 2, stage, ff_half // 2), bf16),
-            vmem((2, 2, stage, ff_half // 2), bf16),
+            vmem((2, 4, stage, ff_half // 2), bf16),
             vmem((2, 2, stage, quarter // 2), bf16),
             vmem((2, 2, stage, quarter // 2), bf16),
             vmem((2, 2, stage, quarter // 2), bf16),
@@ -363,8 +352,8 @@
             vmem((2 * block, quarter), f32),
             vmem((3, rows, quarter), f32),
             pltpu.SemaphoreType.DMA((4,)),
-            pltpu.SemaphoreType.DMA((6,)),
-            sems(nz), sems(nz), sems(nz), sems(nz), sems(nz), sems(2 * nz), sems(8), sems(8),
+            pltpu.SemaphoreType.DMA((12,)),
+            sems(nz), sems(nz), sems(nz), sems(nz), sems(nz), sems(2 * nz), sems(4), sems(4),
             sems(4 * nz), sems(3),
         ],
         compiler_params=pltpu.CompilerParams(

time: 48 us -> 45.8 us (0.954)
  Pallas kernels: 46.3 us -> 44.1 us
    pallas_call x1, Pallas kernels: 46.3 us -> 44.1 us  [fused(): pl.pallas_call(functools.partial(fused_kernel, nz, experts), out_shape=ja...]
where the time goes in v6:
time: 45.8 us; the launch traced here: 45.6 us
  Pallas kernels  44.1 us (96%)
  local copies, waits for them, and re-layouts  1.47 us (3%)
    pallas_call x1, Pallas kernels, fused(): pl.pallas_call(functools.partial(fused_kernel, nz, experts), out_shape=ja...  44.1 us
    unnamed x1, local copies, waits for them, and re-layouts  1.47 us

profile of v6, /device:TPU:0, one launch (start us, length us, event | category | flops | bytes accessed | tf_op | source)
XLA Modules:
  0.0 45.6 jit_solution(9116787456325171838)
XLA Ops:
  0.0 44.1 %shard_map.73 = bf16[8,4096]{1,0:T(8,128)(2,1)} custom-call(bf16[8,4096]{1,0:T(8,128)(2,1)} %tok_hbm.1, s32[8,8]{1,0:T(8,128)} %ids_hbm.1, f32[8,8]{1,0:T(8,128)} %gates_hbm.1, f32[1,4096]{1,0:T(1,128)} %bitcast.1, bf16[1,4096,512]{2,1,0:T(8,128)(2,1)} %wg_hbm.1, bf16[1,4096,512]{2,1,0:T(8,128)(2,1)} %wu_hbm.1, bf16[1,1024,2048]{2,1,0:T(8,128)(2,1)} %wd_hbm.1), custom_call_target="tpu_custom_call" | custom-call | tf_op jit(solution)/shard_map/pallas_call | solution.py:332
  44.1 1.5 %copy.9 = bf16[8,4096]{1,0:T(8,128)(2,1)} copy(bf16[8,4096]{1,0:T(8,128)(2,1)} %shard_map.73) | data formatting | bytes 131072

commit v7 on v6

--- a/solution.py
+++ b/solution.py
@@ -18,8 +18,8 @@
 def fused_kernel(
     nz, experts,
     tok_hbm, ids_hbm, gates_hbm, gain_hbm, wg_hbm, wu_hbm, wd_hbm, out_ref,
-    tok_ref, ids_ref, gates_ref, gain_ref, wgu, wd, xb, lhs, tabs, hid, part_out, part_in, ret_out, ret_in, fin_out, fin_in,
-    t_sem, w_sem, z_sem, x_sem, y_sem, dx_sem, dy_sem, sib_sem, hid_sem, part_sem, ret_sem, fin_sem,
+    tok_ref, ids_ref, gates_ref, gain_ref, wgu, wd, xb, lhs, tabs, hid, part_out, part_in, ret_out, ret_in, near, far_in, fin_out, fin_in,
+    t_sem, w_sem, z_sem, x_sem, y_sem, dx_sem, dy_sem, sib_sem, hid_sem, part_sem, ret_sem, far_sem, fin_sem,
 ):
     f32, bf16 = jnp.float32, jnp.bfloat16
     rows, width = tok_ref.shape
@@ -238,23 +238,44 @@
         for n in range(2):
             hid_copy(chunk, n).wait_recv()
 
-        @pl.loop(0, 2)
-        def _(e):
+        for e in turns(s):
             part_out[s, e, at] = piece_of(chunk, oc, e).astype(bf16)
             part_copy(chunk, e).start()
 
+    def turns(s):
+        return (0, 1) if s else (1, 0)
+
+    parts_y = [slice((1 - m) * stage // 2, (2 - m) * stage // 2) for m in range(2)]
+    y_sum = [
+        remote(ret_out.at[1, 0, at], far_in.at[at], far_sem, m, y_peer) for m, at in enumerate(parts_y)
+    ]
+
     def back_mine(chunk):
         number, s, pairs = chunk
         at = rows_in(pairs)
-
-        @pl.loop(0, 2)
-        def _(e):
+        for e in turns(s):
             own = piece_of(chunk, c, e)
             part_copy(chunk, e).wait_recv()
-            ret_out[s, e, at] = (own + part_in[s, e, at].astype(f32)).astype(bf16)
+            own += part_in[s, e, at].astype(f32)
+            if e == 0 and s == 0:
+                near[...] = own
+                continue
+            ret_out[s, e, at] = own.astype(bf16)
+            if e == 0:
+                for copy in y_sum:
+                    go(copy)
+                continue
             for i in reversed(pairs):
                 if s or i:
                     ret_copy(s, e, i).start()
+
+    def back_near():
+        for m, at in enumerate(parts_y):
+            y_sum[m].wait_recv()
+            ret_out[0, 0, at] = (near[at] + far_in[at].astype(f32)).astype(bf16)
+            for i in reversed(range(nz)):
+                if i and i // (nz // 2) == 1 - m:
+                    ret_copy(0, 0, i).start()
 
     for i in range(nz):
         if i + 1 < nz:
@@ -271,10 +292,11 @@
     for chunk in chunks:
         back_theirs(chunk)
         back_mine(chunk)
-
-    for e in range(2):
+    back_near()
+
+    for e in (1, 0):
         total = ret_out[0, e, pair(0), :].astype(f32)
-        for s in range(2):
+        for s in range(1 + e):
             for i in range(nz):
                 if s or i:
                     ret_copy(s, e, i).wait_recv()
@@ -308,7 +330,7 @@
             hid_copy(chunk, e).wait_send()
             part_copy(chunk, e).wait_send()
             for i in pairs:
-                if s or i:
+                if (s or i) and (e or not s):
                     ret_copy(s, e, i).wait_send()
     for copy in sends:
         copy.wait_send()
@@ -349,12 +371,14 @@
             vmem((2, 2, stage, quarter // 2), bf16),
             vmem((2, 2, stage, quarter // 2), bf16),
             vmem((4 * nz, 2 * block, quarter // 2), bf16),
+            vmem((stage, quarter // 2), f32),
+            vmem((stage, quarter // 2), bf16),
             vmem((2 * block, quarter), f32),
             vmem((3, rows, quarter), f32),
             pltpu.SemaphoreType.DMA((4,)),
             pltpu.SemaphoreType.DMA((12,)),
             sems(nz), sems(nz), sems(nz), sems(nz), sems(nz), sems(2 * nz), sems(4), sems(4),
-            sems(4 * nz), sems(3),
+            sems(4 * nz), sems(2), sems(3),
         ],
         compiler_params=pltpu.CompilerParams(
             collective_id=0, has_side_effects=True, vmem_limit_bytes=56 * 1024 * 1024

time: 45.8 us -> 46.5 us (1.015)
  Pallas kernels: 44.1 us -> 44.8 us
    pallas_call x1, Pallas kernels: 44.1 us -> 44.8 us  [fused(): pl.pallas_call(functools.partial(fused_kernel, nz, experts), out_shape=ja...]
where the time goes in v7:
time: 46.5 us; the launch traced here: 46.3 us
  Pallas kernels  44.8 us (96%)
  local copies, waits for them, and re-layouts  1.47 us (3%)
    pallas_call x1, Pallas kernels, fused(): pl.pallas_call(functools.partial(fused_kernel, nz, experts), out_shape=ja...  44.8 us
    unnamed x1, local copies, waits for them, and re-layouts  1.47 us

profile of v7, /device:TPU:0, one launch (start us, length us, event | category | flops | bytes accessed | tf_op | source)
XLA Modules:
  0.0 46.3 jit_solution(15442855423659824411)
XLA Ops:
  0.0 44.8 %shard_map.73 = bf16[8,4096]{1,0:T(8,128)(2,1)} custom-call(bf16[8,4096]{1,0:T(8,128)(2,1)} %tok_hbm.1, s32[8,8]{1,0:T(8,128)} %ids_hbm.1, f32[8,8]{1,0:T(8,128)} %gates_hbm.1, f32[1,4096]{1,0:T(1,128)} %bitcast.1, bf16[1,4096,512]{2,1,0:T(8,128)(2,1)} %wg_hbm.1, bf16[1,4096,512]{2,1,0:T(8,128)(2,1)} %wu_hbm.1, bf16[1,1024,2048]{2,1,0:T(8,128)(2,1)} %wd_hbm.1), custom_call_target="tpu_custom_call" | custom-call | tf_op jit(solution)/shard_map/pallas_call | solution.py:354
  44.8 1.5 %copy.9 = bf16[8,4096]{1,0:T(8,128)(2,1)} copy(bf16[8,4096]{1,0:T(8,128)(2,1)} %shard_map.73) | data formatting | bytes 131072

commit v8 on v6

--- a/solution.py
+++ b/solution.py
@@ -88,8 +88,6 @@
         greeted += 1
     for load in small:
         load.wait()
-    for load in loads:
-        load.start()
 
     lane = lax.broadcasted_iota(jnp.int32, (rows, LANES), 1)
     table = jnp.zeros((rows, LANES), f32)
@@ -166,6 +164,8 @@
         go(z_copy[i])
     go(x_copy[0])
     go(y_copy[0])
+    for load in loads:
+        load.start()
     def onward(i):
         z_copy[i].wait_recv()
         go(x_copy[i])
@@ -194,20 +194,13 @@
         at = rows_in(pairs)
         return remote(hid.at[s, n, at], hid.at[s, 2 + n, at], hid_sem, 2 * number + n, x_peer)
 
-    def front(chunk):
-        number, s, pairs = chunk
-        at = rows_in(pairs)
-        assemble(s, pairs[-1])
-        if number == 0:
-            for load in loads[:4]:
-                load.wait()
-
-        @pl.loop(0, 2)
-        def _(n):
-            both = dot32(lhs[s, at], wgu[n])
-            gate, up = both[:, :ff_part], both[:, ff_part:]
-            hid[s, n, at] = (gate / (f32(1.0) + jnp.exp(-gate)) * up).astype(bf16)
-            hid_copy(chunk, n).start()
+    def front(chunk, n):
+        number, s, pairs = chunk
+        at = rows_in(pairs)
+        both = dot32(lhs[s, at], wgu[n])
+        gate, up = both[:, :ff_part], both[:, ff_part:]
+        hid[s, n, at] = (gate / (f32(1.0) + jnp.exp(-gate)) * up).astype(bf16)
+        hid_copy(chunk, n).start()
 
     def part_copy(chunk, e):
         number, s, pairs = chunk
@@ -262,12 +255,17 @@
         arrive(i)
         if i:
             assemble(0, i - 1)
-    front(chunks[0])
+    assemble(0, nz - 1)
+    for load in loads[:4]:
+        load.wait()
+    front(chunks[0], 0)
     for i in range(nz):
         arrive_far(i)
-        if i:
-            assemble(1, i - 1)
-    front(chunks[1])
+    front(chunks[0], 1)
+    for i in range(nz):
+        assemble(1, i)
+    for n in range(2):
+        front(chunks[1], n)
     for chunk in chunks:
         back_theirs(chunk)
         back_mine(chunk)

time: 45.8 us -> 47.7 us (1.041)
  Pallas kernels: 44.1 us -> 46 us
    pallas_call x1, Pallas kernels: 44.1 us -> 46 us  [fused(): pl.pallas_call(functools.partial(fused_kernel, nz, experts), out_shape=ja...]
where the time goes in v8:
time: 47.7 us; the launch traced here: 47.5 us
  Pallas kernels  46 us (96%)
  local copies, waits for them, and re-layouts  1.47 us (3%)
    pallas_call x1, Pallas kernels, fused(): pl.pallas_call(functools.partial(fused_kernel, nz, experts), out_shape=ja...  46 us
    unnamed x1, local copies, waits for them, and re-layouts  1.47 us

profile of v8, /device:TPU:0, one launch (start us, length us, event | category | flops | bytes accessed | tf_op | source)
XLA Modules:
  0.0 47.5 jit_solution(7951875469387529951)
XLA Ops:
  0.0 46.0 %shard_map.73 = bf16[8,4096]{1,0:T(8,128)(2,1)} custom-call(bf16[8,4096]{1,0:T(8,128)(2,1)} %tok_hbm.1, s32[8,8]{1,0:T(8,128)} %ids_hbm.1, f32[8,8]{1,0:T(8,128)} %gates_hbm.1, f32[1,4096]{1,0:T(1,128)} %bitcast.1, bf16[1,4096,512]{2,1,0:T(8,128)(2,1)} %wg_hbm.1, bf16[1,4096,512]{2,1,0:T(8,128)(2,1)} %wu_hbm.1, bf16[1,1024,2048]{2,1,0:T(8,128)(2,1)} %wd_hbm.1), custom_call_target="tpu_custom_call" | custom-call | tf_op jit(solution)/shard_map/pallas_call | solution.py:330
  46.0 1.5 %copy.9 = bf16[8,4096]{1,0:T(8,128)(2,1)} copy(bf16[8,4096]{1,0:T(8,128)(2,1)} %shard_map.73) | data formatting | bytes 131072
